TPU v7x, 32 devices: a whole 2x2x4 slice. The times are simulated.
32 devices in a mesh: table: 8 (over z, x), sub: 4 (over y, core).
Axes of the slice: x: 2, y: 2, z: 4, core: 2. Of those that a mesh axis runs over, the one named last changes fastest.
Arguments:
- pooled: bfloat16 [96, 8, 4, 32, 128], P('table', None, 'sub'), may hold values from -6 to 6
- field_owner: int32 [48], replicated, may hold values from 0 to 7, as said below
- w_squeeze: float32 [16, 48], replicated, may hold values from -2.5 to 2.5
- w_excite: float32 [1536, 16], replicated, may hold values from -1.5 to 1.5
- w_bilinear: float32 [32, 32], replicated, may hold values from -1 to 1
- tower_weight: bfloat16 [36096, 1024], P(('table', 'sub')), may hold values from -0.1875 to 0.1875
- tower_cotangent: bfloat16 [1024, 4096], P(None, ('table', 'sub')), may hold values from -6 to 6
Outputs:
- row_grads: bfloat16 [96, 8, 4, 32, 128], P('table', None, 'sub')
- tower_weight_grad: float32 [36096, 1024], P(('table', 'sub'))
- squeeze_grad: float32 [16, 48], replicated
- excite_grad: float32 [1536, 16], replicated
- bilinear_grad: float32 [32, 32], replicated
Inputs may be any that keep to these rules, and one draw needn't show every extreme that they name: `field_owner`: each table index holds at most 12 fields, and some index holds exactly 12.
All inputs are finite; a program needn't handle non-finite values.
Results may differ from a plain program's by a relative error of at most 0.0074.
Values may be sent and summed in bfloat16 or wider, within the bound.
A program may use at most 192 MiB of HBM per device.

v0:
```python
import jax
import jax.numpy as jnp
from jax import lax
from jax.sharding import PartitionSpec as P


def hadamard_table(width):
    index = jnp.arange(width, dtype=jnp.int32)
    both = index[:, None] & index[None, :]
    parity = jnp.zeros((width, width), jnp.int32)
    for bit_pos in range(width.bit_length()):
        parity = parity ^ both >> bit_pos & 1
    return (1 - 2 * parity).astype(jnp.bfloat16)


def slot_table(field_owner, per_owner):
    count = field_owner.shape[0]
    order = jnp.arange(count, dtype=jnp.int32)
    same = field_owner[:, None] == field_owner[None, :]
    earlier = order[:, None] > order[None, :]
    position = jnp.sum((same & earlier).astype(jnp.int32), axis=1)
    return field_owner * per_owner + position


def forward(fields, w_squeeze, w_excite, w_bilinear):
    count, width, samples = fields.shape
    high = lax.Precision.HIGHEST
    squeezed = jnp.mean(fields, axis=1)
    activated = jax.nn.silu(jnp.dot(w_squeeze, squeezed, precision=high))
    excite = jnp.dot(w_excite, activated, precision=high).reshape(count, width, samples)
    weighted = fields * (1.0 + excite)
    mapped = jnp.einsum("ed,fen->fdn", w_bilinear, weighted, precision=high)
    pieces = [mapped[left][None] * weighted[left + 1 :] for left in range(count - 1)]
    pairs = jnp.concatenate(pieces, axis=0)
    return pairs.reshape(-1, samples).astype(jnp.bfloat16)


def tower_step(pair_cols, weights, piece):
    total = lax.dot_general(
        pair_cols, piece, (((1,), (1,)), ((), ())), preferred_element_type=jnp.float32
    )
    block = jnp.dot(weights, piece, preferred_element_type=jnp.float32).astype(jnp.bfloat16)
    return (total, block)


def on_device(pooled, field_owner, w_squeeze, w_excite, w_bilinear, tower_weight, tower_cotangent):
    per_owner = pooled.shape[0]
    width = pooled.shape[3]
    samples = pooled.shape[4]
    tables = lax.axis_size("table")
    total_samples = tables * lax.axis_size("sub") * samples
    scale = 1.0 / width**0.5
    signs = hadamard_table(width)
    rotated = (
        jnp.einsum("ij,ktsjb->ktsib", signs, pooled, preferred_element_type=jnp.float32) * scale
    ).astype(jnp.bfloat16)
    received = lax.all_to_all(rotated, "table", split_axis=1, concat_axis=0, tiled=True)
    received = received.reshape(per_owner * tables, width, samples)
    slot_index = slot_table(field_owner, per_owner)
    selected = jnp.take(received, slot_index, axis=0)
    fields = jnp.einsum("ij,fjn->fin", signs, selected, preferred_element_type=jnp.float32) * scale
    pairs, back = jax.vjp(forward, fields, w_squeeze, w_excite, w_bilinear)
    pair_cols = lax.all_to_all(pairs, ("table", "sub"), split_axis=0, concat_axis=1, tiled=True)
    weight_total, grads = tower_step(
        pair_cols,
        tower_weight,
        lax.all_gather(tower_cotangent, ("table", "sub"), axis=1, tiled=True),
    )
    pair_grad = lax.all_to_all(grads, ("table", "sub"), split_axis=1, concat_axis=0, tiled=True)
    field_grad, d_squeeze, d_excite, d_bilinear = back(pair_grad)
    g_squeeze, g_excite, g_bilinear = lax.psum((d_squeeze, d_excite, d_bilinear), ("table", "sub"))
    slot_count = per_owner * tables
    onehot = (slot_index[None, :] == jnp.arange(slot_count, dtype=jnp.int32)[:, None]).astype(
        jnp.bfloat16
    )
    placed = jnp.einsum(
        "sf,fen->sen", onehot, field_grad.astype(jnp.bfloat16), preferred_element_type=jnp.float32
    ).astype(jnp.bfloat16)
    placed = placed.reshape(slot_count, 1, 1, width, samples)
    row_grads = lax.all_to_all(placed, "table", split_axis=0, concat_axis=1, tiled=True)
    inverse = 1.0 / total_samples
    return (
        row_grads,
        weight_total * inverse,
        g_squeeze * inverse,
        g_excite * inverse,
        g_bilinear * inverse,
    )


def solution(mesh):
    return jax.shard_map(
        on_device,
        mesh=mesh,
        in_specs=(
            P("table", None, "sub", None, None),
            P(),
            P(),
            P(),
            P(),
            P(("table", "sub"), None),
            P(None, ("table", "sub")),
        ),
        out_specs=(P("table", None, "sub", None, None), P(("table", "sub"), None), P(), P(), P()),
        check_vma=False,
    )
```

profile of v0, /device:TPU:0, one launch (start us, length us, event | category | flops | bytes accessed | tf_op | source)
XLA Modules:
  0.0 775.6 jit_solution(4471121954615610311)
XLA Ops:
  7.9 1.5 fusion.4
  10.4 7.2 all-to-all-start
  17.6 92.7 %all-gather.2.cloned.1.call-done = bf16[1024,4096]{1,0:T(8,128)(2,1)} async-done(((bf16[1024,128]{1,0:T(8,128)(2,1)}), bf16[1024,4096]{1,0:T(8,128)(2,1)}) %all-gather.2.cloned.1.call-update) | async-done | bytes 8388624 | tf_op jit(solution)/shard_map/all_gather | solution.py:67
  110.3 15.1 %fusion = bf16[141,32,8,128]{3,2,1,0:T(8,128)(2,1)} fusion(bf16[1128,1024]{1,0:T(8,128)(2,1)S(1)} %copy-done, bf16[1024,4096]{1,0:T(8,128)(2,1)} %all-gather.2.cloned.1.call-done), kind=kOutput, calls=%fused_computation.3 | convolution fusion | flops 9466970112 | bytes 19939328 | tf_op jit(solution)/shard_map/dot_general | solution.py:42
  125.4 8.8 %copy.48 = bf16[141,32,8,128]{3,2,0,1:T(8,128)(2,1)} copy(bf16[141,32,8,128]{3,2,1,0:T(8,128)(2,1)} %fusion) | data formatting | bytes 18481152 | tf_op jit(solution)/shard_map/all_to_all | solution.py:69
  134.3 4.0 all-to-all-start.1
  144.5 197.3 %all-to-all-done.1 = bf16[1128,32,128]{2,0,1:T(8,128)(2,1)} async-done(((bf16[1128,32,128]{2,0,1:T(8,128)(2,1)}), bf16[1128,32,128]{2,0,1:T(8,128)(2,1)}, u32[]{:S(2)}, u32[]{:S(2)}) %all-to-all-start.1) | async-done | bytes 9240608 | tf_op jit(solution)/shard_map/all_to_all | solution.py:69
  341.8 11.1 %convert_element_type.58 = f32[1128,32,128]{2,0,1:T(8,128)} convert(bf16[1128,32,128]{2,0,1:T(8,128)(2,1)} %all-to-all-done.1) | non-fusion elementwise | flops 4620288 | bytes 27721728 | tf_op jit(solution)/shard_map/transpose(jvp())/convert_element_type | solution.py:35
  405.4 2.0 multiply_reduce_fusion.34
  418.3 1.4 multiply_reduce_fusion.24
  424.0 1.4 multiply_reduce_fusion.20
  426.1 1.5 multiply_reduce_fusion.18
  427.6 1.5 multiply_reduce_fusion.17
  433.5 1.5 multiply_reduce_fusion.9
  440.0 13.2 %fusion.87 = (f32[48,32,128]{2,1,0:T(8,128)S(1)}, f32[48,32,128]{2,1,0:T(8,128)S(1)}) fusion(f32[48,32,128]{2,1,0:T(8,128)S(1)} %copy-done.5, f32[32,32]{1,0:T(8,128)} %param.11, f32[1,32,128]{2,1,0:T(8,128)} %bitcast.400, f32[1,32,128]{2,1,0:T(8,128)S(1)} %bitcast.452, f32[1,32,128]{2,1,0:T(8,128)S(1)} %bitcast.450, f32[1,32,128]{2,1,0:T(8,128)} %bitcast.448, ...), kind=kOutput, calls=%fused_computation.312 | convolution fusion | flops 93978624 | bytes 21614592 | tf_op jit(solution)/shard_map/transpose(jvp(ed,fen->fdn))/dot_general | solution.py:32
  456.1 3.7 all-to-all-start.2
  466.4 1.5 fusion.22
  470.2 1.5 fusion.26
  496.1 10.3 %all-to-all-start.3 = ((bf16[32,1128,128]{2,1,0:T(8,128)(2,1)}), bf16[32,1128,128]{2,1,0:T(8,128)(2,1)}, u32[]{:S(2)}, u32[]{:S(2)}) async-start(bf16[32,1128,128]{2,1,0:T(8,128)(2,1)} %bitcast.344), calls=%async_computation.3 | async-start | bytes 18481152 | tf_op jit(solution)/shard_map/all_to_all | solution.py:63
  508.7 1.7 convolution_bitcast_fusion.2
  510.4 226.3 %all-reduce.94 = (f32[16,48]{1,0:T(8,128)S(1)}, f32[32,32]{1,0:T(8,128)S(1)}) all-reduce(f32[16,48]{1,0:T(8,128)S(1)} %fusion.53, f32[32,32]{1,0:T(8,128)S(1)} %convolution_bitcast_fusion.2), channel_id=1, replica_groups=mesh['table'=8,'sub'=4] {'table','sub'}, use_global_device_ids=true, to_apply=%region_48.49 | all-reduce | flops 1792 | bytes 14336 | tf_op jit(solution)/shard_map/psum | solution.py:71
  737.9 1.5 broadcast_multiply_fusion.41
  740.4 12.3 %copy.39 = bf16[1128,32,128]{0,2,1:T(8,128)(2,1)} copy(bf16[1128,32,128]{2,0,1:T(8,128)(2,1)} %bitcast.170) | data formatting | bytes 18481152 | tf_op jit(solution)/shard_map/all_to_all | solution.py:63
  752.7 16.0 %convolution_multiply_fusion = f32[1128,1024]{1,0:T(8,128)} fusion(bf16[1128,4096]{0,1:T(8,128)(2,1)} %bitcast.345, bf16[1024,4096]{1,0:T(8,128)(2,1)} %all-gather.2.cloned.1.call-done), kind=kOutput, calls=%fused_computation.4 | convolution fusion | flops 9463504896 | bytes 22249472 | tf_op jit(solution)/shard_map/dot_general | solution.py:39
  (459 shorter events, 124.7 us)
Async XLA Ops:
  7.2 103.2 %all-gather.2.cloned.1.call-start = ((), (), s32[]{:S(2)}) async-start(), calls=%async_computation.4 | async-start | bytes 8650752 | tf_op jit(solution)/shard_map/all_gather | solution.py:67
  10.4 123.9 %all-to-all-start = ((bf16[12,8,1,32,128]{4,3,0,2,1:T(8,128)(2,1)}), bf16[12,8,1,32,128]{4,3,0,2,1:T(8,128)(2,1)S(1)}, u32[]{:S(2)}, u32[]{:S(2)}) async-start(bf16[12,8,1,32,128]{4,3,0,2,1:T(8,128)(2,1)} %copy.33), calls=%async_computation | async-start | bytes 1572864 | tf_op jit(solution)/shard_map/all_to_all | solution.py:57
  134.3 207.5 %all-to-all-start.1 = ((bf16[1128,32,128]{2,0,1:T(8,128)(2,1)}), bf16[1128,32,128]{2,0,1:T(8,128)(2,1)}, u32[]{:S(2)}, u32[]{:S(2)}) async-start(bf16[1128,32,128]{2,0,1:T(8,128)(2,1)} %bitcast.343), calls=%async_computation.1 | async-start | bytes 18481152 | tf_op jit(solution)/shard_map/all_to_all | solution.py:69
  143.6 255.3 %copy-start.68 = (f32[32,128]{1,0:T(8,128)}, f32[32,128]{1,0:T(8,128)S(1)}, u32[]{:S(2)}) copy-start(f32[32,128]{1,0:T(8,128)S(1)} %get-tuple-element.68) | copy-start | bytes 49156
  143.7 256.5 %copy-start.92 = (f32[32,128]{1,0:T(8,128)}, f32[32,128]{1,0:T(8,128)S(1)}, u32[]{:S(2)}) copy-start(f32[32,128]{1,0:T(8,128)S(1)} %get-tuple-element.66) | copy-start | bytes 49156
  143.7 257.8 %copy-start.70 = (f32[32,128]{1,0:T(8,128)}, f32[32,128]{1,0:T(8,128)S(1)}, u32[]{:S(2)}) copy-start(f32[32,128]{1,0:T(8,128)S(1)} %get-tuple-element.65) | copy-start | bytes 49156
  143.7 259.1 %copy-start.72 = (f32[32,128]{1,0:T(8,128)}, f32[32,128]{1,0:T(8,128)S(1)}, u32[]{:S(2)}) copy-start(f32[32,128]{1,0:T(8,128)S(1)} %get-tuple-element.64) | copy-start | bytes 49156
  143.7 260.4 %copy-start.74 = (f32[32,128]{1,0:T(8,128)}, f32[32,128]{1,0:T(8,128)S(1)}, u32[]{:S(2)}) copy-start(f32[32,128]{1,0:T(8,128)S(1)} %get-tuple-element.63) | copy-start | bytes 49156
  143.7 263.7 %copy-start.76 = (f32[32,128]{1,0:T(8,128)}, f32[32,128]{1,0:T(8,128)S(1)}, u32[]{:S(2)}) copy-start(f32[32,128]{1,0:T(8,128)S(1)} %get-tuple-element.61) | copy-start | bytes 49156
  144.4 264.4 %copy-start.78 = (f32[32,128]{1,0:T(8,128)}, f32[32,128]{1,0:T(8,128)S(1)}, u32[]{:S(2)}) copy-start(f32[32,128]{1,0:T(8,128)S(1)} %get-tuple-element.59) | copy-start | bytes 49156
  144.4 265.7 %copy-start.90 = (f32[32,128]{1,0:T(8,128)}, f32[32,128]{1,0:T(8,128)S(1)}, u32[]{:S(2)}) copy-start(f32[32,128]{1,0:T(8,128)S(1)} %get-tuple-element.57) | copy-start | bytes 49156
  144.4 267.1 %copy-start.30 = (f32[32,128]{1,0:T(8,128)}, f32[32,128]{1,0:T(8,128)S(1)}, u32[]{:S(2)}) copy-start(f32[32,128]{1,0:T(8,128)S(1)} %get-tuple-element.56) | copy-start | bytes 49156
  144.4 268.4 %copy-start.82 = (f32[32,128]{1,0:T(8,128)}, f32[32,128]{1,0:T(8,128)S(1)}, u32[]{:S(2)}) copy-start(f32[32,128]{1,0:T(8,128)S(1)} %get-tuple-element.55) | copy-start | bytes 49156
  144.4 269.8 %copy-start.32 = (f32[32,128]{1,0:T(8,128)}, f32[32,128]{1,0:T(8,128)S(1)}, u32[]{:S(2)}) copy-start(f32[32,128]{1,0:T(8,128)S(1)} %get-tuple-element.54) | copy-start | bytes 49156
  144.4 271.1 %copy-start.34 = (f32[32,128]{1,0:T(8,128)}, f32[32,128]{1,0:T(8,128)S(1)}, u32[]{:S(2)}) copy-start(f32[32,128]{1,0:T(8,128)S(1)} %get-tuple-element.53) | copy-start | bytes 49156
  144.4 272.5 %copy-start.36 = (f32[32,128]{1,0:T(8,128)}, f32[32,128]{1,0:T(8,128)S(1)}, u32[]{:S(2)}) copy-start(f32[32,128]{1,0:T(8,128)S(1)} %get-tuple-element.52) | copy-start | bytes 49156
  144.4 273.9 %copy-start.38 = (f32[32,128]{1,0:T(8,128)}, f32[32,128]{1,0:T(8,128)S(1)}, u32[]{:S(2)}) copy-start(f32[32,128]{1,0:T(8,128)S(1)} %get-tuple-element.51) | copy-start | bytes 49156
  144.4 275.3 %copy-start.40 = (f32[32,128]{1,0:T(8,128)}, f32[32,128]{1,0:T(8,128)S(1)}, u32[]{:S(2)}) copy-start(f32[32,128]{1,0:T(8,128)S(1)} %get-tuple-element.50) | copy-start | bytes 49156
  144.4 276.7 %copy-start.42 = (f32[32,128]{1,0:T(8,128)}, f32[32,128]{1,0:T(8,128)S(1)}, u32[]{:S(2)}) copy-start(f32[32,128]{1,0:T(8,128)S(1)} %get-tuple-element.49) | copy-start | bytes 49156
  144.5 278.1 %copy-start.44 = (f32[32,128]{1,0:T(8,128)}, f32[32,128]{1,0:T(8,128)S(1)}, u32[]{:S(2)}) copy-start(f32[32,128]{1,0:T(8,128)S(1)} %get-tuple-element.48) | copy-start | bytes 49156
  144.5 279.5 %copy-start.46 = (f32[32,128]{1,0:T(8,128)}, f32[32,128]{1,0:T(8,128)S(1)}, u32[]{:S(2)}) copy-start(f32[32,128]{1,0:T(8,128)S(1)} %get-tuple-element.47) | copy-start | bytes 49156
  456.1 39.6 %all-to-all-start.2 = ((bf16[96,1,1,32,128]{4,3,2,1,0:T(8,128)(2,1)}), bf16[96,1,1,32,128]{4,3,2,1,0:T(8,128)(2,1)S(1)}, u32[]{:S(2)}, u32[]{:S(2)}) async-start(bf16[96,1,1,32,128]{4,3,2,1,0:T(8,128)(2,1)} %copy.38), calls=%async_computation.2 | async-start | bytes 1572864 | tf_op jit(solution)/shard_map/all_to_all | solution.py:80
  496.1 244.3 %all-to-all-start.3 = ((bf16[32,1128,128]{2,1,0:T(8,128)(2,1)}), bf16[32,1128,128]{2,1,0:T(8,128)(2,1)}, u32[]{:S(2)}, u32[]{:S(2)}) async-start(bf16[32,1128,128]{2,1,0:T(8,128)(2,1)} %bitcast.344), calls=%async_computation.3 | async-start | bytes 18481152 | tf_op jit(solution)/shard_map/all_to_all | solution.py:63
  506.4 231.5 %all-reduce.97.cloned.1.call-start = ((), (), s32[]{:S(2)}) async-start(), calls=%async_computation.5 | async-start | bytes 196608 | tf_op jit(solution)/shard_map/psum | solution.py:71
  (127 other events, 4738.9 us)
Sparse Core Ops, SparseCore 0:
  10.9 99.4 all-gather.1
  513.4 200.6 all-reduce.96
where the time goes:
time: 778 us; the launch traced here: 776 us
  waiting for transfers between devices  291 us (37%)
  blocking collectives  226 us (29%)
  other arithmetic  104 us (13%)
  local copies, waits for them, and re-layouts  61.3 us (8%)
  matrix products  52.5 us (7%)
  starting transfers between devices  25.6 us (3%)
  between operations  15.7 us (2%)
    psum x1, blocking collectives, on_device(): lax.psum((d_squeeze, d_excite, d_bilinear), ('table', 'sub'))  226 us
    all_to_all x1, waiting for transfers between devices, on_device(): lax.all_to_all(grads, ('table', 'sub'), split_axis=1, concat_axis=0, tile...  197 us
    all_gather x1, waiting for transfers between devices, on_device(): lax.all_gather(tower_cotangent, ('table', 'sub'), axis=1, tiled=True)  92.7 us
    reduce_sum x46, other arithmetic, forward(): mapped[left][None] * weighted[left + 1:]  48.5 us
    unnamed x46, other arithmetic  35.2 us
    split x46, local copies, waits for them, and re-layouts, forward(): pairs = jnp.concatenate(pieces, axis=0)  33.1 us
    dot_general x1, matrix products, tower_step(): lax.dot_general(pair_cols, piece, (((1,), (1,)), ((), ())), preferred_ele...  16 us
    dot_general x3, matrix products, forward(): mapped = jnp.einsum('ed,fen->fdn', w_bilinear, weighted, precision=high)  15.7 us
  transfers between devices with their start and end apart: 6, of which 2 were waited for; matrix products, arithmetic and copies ran while one was open for 9% of the time, Pallas kernels for 0%

commit v1 on v0

v1 whole, which is shorter than its diff:
```python
import functools

import jax
import jax.numpy as jnp
import numpy as np
from jax import lax
from jax.experimental import pallas as pl
from jax.experimental.pallas import tpu as pltpu
from jax.sharding import Mesh
from jax.sharding import PartitionSpec as P

HIGH = lax.Precision.HIGHEST
TABLE = ("a", "l")
GROUP = ("l", "sub")
EVERY = ("a", "l", "sub")


def hadamard_table(width):
    index = jnp.arange(width, dtype=jnp.int32)
    both = index[:, None] & index[None, :]
    parity = jnp.zeros((width, width), jnp.int32)
    for bit_pos in range(width.bit_length()):
        parity = parity ^ both >> bit_pos & 1
    return (1 - 2 * parity).astype(jnp.bfloat16)


def slot_table(field_owner, per_owner):
    count = field_owner.shape[0]
    order = jnp.arange(count, dtype=jnp.int32)
    same = field_owner[:, None] == field_owner[None, :]
    earlier = order[:, None] > order[None, :]
    position = jnp.sum((same & earlier).astype(jnp.int32), axis=1)
    return field_owner * per_owner + position


def bits_of(size):
    return [1 << k for k in range(size.bit_length() - 1)]


def swap(x, size, bit):
    return lax.ppermute(x, GROUP, [(d, d ^ bit) for d in range(size)])


def gather_rows(shard, size, me):
    held = shard[None]
    offsets = [0]
    for bit in reversed(bits_of(size)):
        held = jnp.concatenate([held, swap(held, size, bit)], axis=0)
        offsets = offsets + [o ^ bit for o in offsets]
    place = np.argsort(np.array(offsets))
    order = jnp.asarray(place, jnp.int32)[jnp.arange(size, dtype=jnp.int32) ^ me]
    parts = [lax.dynamic_index_in_dim(held, order[d], 0, keepdims=False) for d in range(size)]
    return jnp.concatenate(parts, axis=0)


def scatter_rows(total, size, me):
    held = total.reshape(size, total.shape[0] // size, total.shape[1])
    result = None
    for bit in bits_of(size):
        half = held.shape[0] // 2
        view = held.reshape(half, 2, held.shape[1], held.shape[2])
        side = lax.rem(me // bit, 2)
        keep = lax.dynamic_index_in_dim(view, side, 1, keepdims=False)
        give = lax.dynamic_index_in_dim(view, 1 - side, 1, keepdims=False)
        got = swap(give, size, bit)
        result = keep.astype(jnp.float32) + got.astype(jnp.float32)
        held = result.astype(jnp.bfloat16)
    return result[0] if result is not None else held[0].astype(jnp.float32)


def tower_kernel(
    chunk, left_ref, right_ref, w_ref, cot_ref, wt_ref, fwd_ref, bwd_ref,
    twg_ref, dwt_ref, gb_ref, cot2, mf, dm, dw, pg, prs,
):
    parts, count, width, lanes = wt_ref.shape
    step = pl.program_id(0)
    depth = cot2.shape[0]
    tile = min(256, depth)
    ntile = min(256, parts * lanes)

    def columns(a):
        return slice(a * lanes, (a + 1) * lanes)

    @pl.when(step == 0)
    def _():
        for a in range(parts):
            cot2[:, columns(a)] = cot_ref[a]

        @pl.loop(0, count)
        def _(f):
            rows = jnp.concatenate([wt_ref[a, f] for a in range(parts)], axis=1)
            both = jnp.dot(fwd_ref[...], rows, preferred_element_type=jnp.float32)
            value = both[:width] + both[width:]
            for a in range(parts):
                mf[a, f] = value[:, columns(a)]
                dm[a, f] = jnp.zeros((width, lanes), jnp.float32)
                dw[a, f] = jnp.zeros((width, lanes), jnp.float32)

    @pl.loop(0, parts * lanes // ntile)
    def _(c):
        cols = pl.ds(pl.multiple_of(c * ntile, ntile), ntile)
        pg[:, cols] = jnp.dot(w_ref[...], cot2[:, cols], preferred_element_type=jnp.float32)

    @pl.loop(0, chunk)
    def _(q):
        i = left_ref[step * chunk + q]
        j = right_ref[step * chunk + q]
        rows = pl.ds(pl.multiple_of(q * width, width), width)
        for a in range(parts):
            g = pg[rows, columns(a)]
            w = wt_ref[a, j].astype(jnp.float32)
            m = mf[a, i]
            prs[rows, columns(a)] = (m * w).astype(jnp.bfloat16)
            dm[a, i] += g * w
            dw[a, j] += g * m

    @pl.loop(0, depth // tile)
    def _(c):
        cols = pl.ds(pl.multiple_of(c * tile, tile), tile)
        twg_ref[:, cols] = lax.dot_general(
            prs[...], cot2[cols, :], (((1,), (1,)), ((), ())), preferred_element_type=jnp.float32
        ).astype(jnp.bfloat16)

    @pl.when(step == pl.num_programs(0) - 1)
    def _():
        gb_ref[...] = jnp.zeros_like(gb_ref)

        @pl.loop(0, count)
        def _(f):
            d = jnp.concatenate([dm[a, f].astype(jnp.bfloat16) for a in range(parts)], axis=1)
            rows = jnp.concatenate([wt_ref[a, f] for a in range(parts)], axis=1)
            both = jnp.dot(bwd_ref[...], d, preferred_element_type=jnp.float32)
            value = both[:width] + both[width:]
            for a in range(parts):
                dwt_ref[a, f] = (dw[a, f] + value[:, columns(a)]).astype(jnp.bfloat16)
            gb_ref[...] += lax.dot_general(
                rows, d, (((1,), (1,)), ((), ())), preferred_element_type=jnp.float32
            )


def two_parts(matrix):
    top = matrix.astype(jnp.bfloat16)
    rest = (matrix - top.astype(jnp.float32)).astype(jnp.bfloat16)
    return jnp.concatenate([top, rest], axis=0)


def tower_step(left, right, weights, cot, weighted, w_bilinear):
    parts, count, width, lanes = weighted.shape
    depth = cot.shape[1]
    pairs = left.shape[0]
    steps = next(c for c in (3, 2, 4, 5, 6, 7, 1) if pairs % c == 0)
    chunk = pairs // steps
    rows = chunk * width
    samples = parts * lanes

    def whole(shape):
        return pl.BlockSpec(shape, lambda s, *_: (0,) * len(shape), pipeline_mode=pl.Buffered(1))

    big = (parts, count, width, lanes)
    return pl.pallas_call(
        functools.partial(tower_kernel, chunk),
        grid_spec=pltpu.PrefetchScalarGridSpec(
            num_scalar_prefetch=2,
            grid=(steps,),
            in_specs=[
                pl.BlockSpec((rows, depth), lambda s, *_: (s, 0)),
                whole(cot.shape),
                whole(big),
                whole((2 * width, width)),
                whole((2 * width, width)),
            ],
            out_specs=[
                pl.BlockSpec((rows, depth), lambda s, *_: (s, 0)),
                whole(big),
                whole((width, width)),
            ],
            scratch_shapes=[
                pltpu.VMEM((depth, samples), jnp.bfloat16),
                pltpu.VMEM(big, jnp.float32),
                pltpu.VMEM(big, jnp.float32),
                pltpu.VMEM(big, jnp.float32),
                pltpu.VMEM((rows, samples), jnp.float32),
                pltpu.VMEM((rows, samples), jnp.bfloat16),
            ],
        ),
        out_shape=[
            jax.ShapeDtypeStruct((pairs * width, depth), jnp.bfloat16),
            jax.ShapeDtypeStruct(big, jnp.bfloat16),
            jax.ShapeDtypeStruct((width, width), jnp.float32),
        ],
        compiler_params=pltpu.CompilerParams(
            dimension_semantics=("arbitrary",), vmem_limit_bytes=60 * 1024 * 1024
        ),
        cost_estimate=pl.CostEstimate(
            flops=4 * pairs * width * depth * samples,
            bytes_accessed=4 * pairs * width * depth,
            transcendentals=0,
        ),
    )(left, right, weights, cot, weighted, two_parts(w_bilinear.T), two_parts(w_bilinear))


def on_device(pooled, field_owner, w_squeeze, w_excite, w_bilinear, tower_weight, tower_cotangent):
    per_owner, width, samples = pooled.shape[0], pooled.shape[3], pooled.shape[4]
    count = field_owner.shape[0]
    hidden = w_squeeze.shape[0]
    parts, locals_, subs = lax.axis_size("a"), lax.axis_size("l"), lax.axis_size("sub")
    tables = parts * locals_
    size = locals_ * subs
    me = lax.axis_index("l") * subs + lax.axis_index("sub")
    scale = 1.0 / width**0.5
    signs = hadamard_table(width)

    weights = gather_rows(tower_weight, size, me)
    cot = lax.all_gather(tower_cotangent, "a", axis=0, tiled=False)

    rotated = (
        jnp.einsum("ij,ktsjb->ktsib", signs, pooled, preferred_element_type=jnp.float32) * scale
    ).astype(jnp.bfloat16)
    received = lax.all_to_all(rotated, TABLE, split_axis=1, concat_axis=0, tiled=True)
    received = received.reshape(per_owner * tables, width, samples)
    slot_index = slot_table(field_owner, per_owner)
    selected = jnp.take(received, slot_index, axis=0)
    fields = jnp.einsum("ij,fjn->fin", signs, selected, preferred_element_type=jnp.float32) * scale
    squeezed = jnp.mean(fields, axis=1)
    raw = jnp.dot(w_squeeze, squeezed, precision=HIGH)
    gate = jax.nn.sigmoid(raw)
    activated = raw * gate
    excite = jnp.dot(w_excite, activated, precision=HIGH).reshape(count, width, samples)
    weighted = fields * (1.0 + excite)
    weighted_all = lax.all_gather(weighted.astype(jnp.bfloat16), "a", axis=0, tiled=False)

    table_left, table_right = np.triu_indices(count, 1)
    mine = table_left.shape[0] // parts
    start = lax.axis_index("a") * mine
    left = lax.dynamic_slice_in_dim(jnp.asarray(table_left, jnp.int32), start, mine)
    right = lax.dynamic_slice_in_dim(jnp.asarray(table_right, jnp.int32), start, mine)
    totals, partial, d_bilinear = tower_step(left, right, weights, cot, weighted_all, w_bilinear)

    arrived = lax.all_to_all(partial, "a", split_axis=0, concat_axis=0, tiled=True)
    d_weighted = jnp.sum(arrived.astype(jnp.float32), axis=0)
    weight_total = scatter_rows(totals, size, me)

    d_excite = (d_weighted * fields).reshape(count * width, samples)
    g_excite = lax.dot_general(activated, d_excite, (((1,), (1,)), ((), ())), precision=HIGH)
    d_act = lax.dot_general(w_excite, d_excite, (((0,), (0,)), ((), ())), precision=HIGH)
    d_raw = d_act * (gate * (1.0 + raw * (1.0 - gate)))
    g_squeeze = lax.dot_general(d_raw, squeezed, (((1,), (1,)), ((), ())), precision=HIGH)
    d_squeezed = lax.dot_general(w_squeeze, d_raw, (((0,), (0,)), ((), ())), precision=HIGH)
    field_grad = d_weighted * (1.0 + excite) + (d_squeezed * (1.0 / width))[:, None, :]

    flat = jnp.concatenate([g_excite.reshape(-1), g_squeeze.reshape(-1), d_bilinear.reshape(-1)])
    flat = jnp.pad(flat, (0, -flat.shape[0] % 1024)).reshape(-1, 128)
    inverse = 1.0 / (tables * subs * samples)
    flat = (lax.psum(flat, EVERY) * inverse).reshape(-1)
    n_excite, n_squeeze = count * width * hidden, hidden * count
    g_excite = flat[:n_excite].reshape(hidden, count * width).T
    g_squeeze = flat[n_excite : n_excite + n_squeeze].reshape(hidden, count)
    at = n_excite + n_squeeze
    g_bilinear = flat[at : at + width * width].reshape(width, width)

    slot_count = per_owner * tables
    onehot = (slot_index[None, :] == jnp.arange(slot_count, dtype=jnp.int32)[:, None]).astype(
        jnp.bfloat16
    )
    placed = jnp.einsum(
        "sf,fen->sen", onehot, field_grad.astype(jnp.bfloat16), preferred_element_type=jnp.float32
    ).astype(jnp.bfloat16)
    placed = placed.reshape(slot_count, 1, 1, width, samples)
    row_grads = lax.all_to_all(placed, TABLE, split_axis=0, concat_axis=1, tiled=True)
    return (row_grads, weight_total * inverse, g_squeeze, g_excite, g_bilinear)


def solution(mesh):
    tables, subs = mesh.shape["table"], mesh.shape["sub"]

    def run(pooled, field_owner, *rest):
        count = field_owner.shape[0]
        pairs = count * (count - 1) // 2
        parts = max(a for a in range(1, tables + 1) if tables % a == 0 and pairs % a == 0)
        fine = Mesh(mesh.devices.reshape(parts, tables // parts, subs), EVERY)
        return jax.shard_map(
            on_device,
            mesh=fine,
            in_specs=(
                P(TABLE, None, "sub", None, None),
                P(),
                P(),
                P(),
                P(),
                P(EVERY, None),
                P(None, EVERY),
            ),
            out_specs=(P(TABLE, None, "sub", None, None), P(EVERY, None), P(), P(), P()),
            check_vma=False,
        )(pooled, field_owner, *rest)

    return run
```

time: 778 us -> 428 us (0.55)
  blocking collectives: 226 us -> 0 us
  other arithmetic: 104 us -> 34 us
  Pallas kernels: 0 us -> 53.9 us
  matrix products: 52.5 us -> 5.54 us
  local copies, waits for them, and re-layouts: 61.3 us -> 26.4 us
  waiting for transfers between devices: 291 us -> 266 us
    psum x1 -> x0, blocking collectives: 226 us -> none  [on_device(): lax.psum((d_squeeze, d_excite, d_bilinear), ('table', 'sub'))]
    all_to_all x4 -> x3, waiting for transfers between devices: 197 us -> 56.8 us  [the longest x1 56.8 us: on_device(): lax.all_to_all(partial, 'a', split_axis=0, concat_axis=0, tiled=True)]
    psum x1, waiting for transfers between devices: 0.01 us -> 127 us  [on_device(): flat = (lax.psum(flat, EVERY) * inverse).reshape(-1)]
    all_gather x1 -> x2, waiting for transfers between devices: 92.7 us -> 35.2 us  [the longest x1 35.2 us: on_device(): lax.all_gather(weighted.astype(jnp.bfloat16), 'a', axis=0, tiled=False)]
    pallas_call x0 -> x1, Pallas kernels: none -> 53.9 us  [tower_step(): pl.pallas_call(functools.partial(tower_kernel, chunk), grid_spec=pltpu.Pr...]
    ppermute x0 -> x4, waiting for transfers between devices: none -> 46.7 us  [swap(): return lax.ppermute(x, GROUP, [(d, d ^ bit) for d in range(size)])]
    dot_general x11 -> x6, matrix products: 50.2 us -> 3.51 us  [the longest x1 1.73 us: on_device(): jnp.dot(w_excite, activated, precision=HIGH).reshape(count, width, samples)]
    reduce_sum x46 -> x1, other arithmetic: 48.5 us -> 2.42 us  [on_device(): d_weighted = jnp.sum(arrived.astype(jnp.float32), axis=0)]
  transfers between devices with their start and end apart: 6 -> 10, of which waited for: 2 -> 5; matrix products, arithmetic and copies ran while one was open for 9% -> 12% of each run, Pallas kernels for 0% -> 0%
where the time goes in v1:
time: 428 us; the launch traced here: 427 us
  waiting for transfers between devices  266 us (62%)
  Pallas kernels  53.9 us (13%)
  other arithmetic  34 us (8%)
  local copies, waits for them, and re-layouts  26.4 us (6%)
  between operations  22 us (5%)
  starting transfers between devices  18.7 us (4%)
  matrix products  5.54 us (1%)
    psum x1, waiting for transfers between devices, on_device(): flat = (lax.psum(flat, EVERY) * inverse).reshape(-1)  127 us
    all_to_all x1, waiting for transfers between devices, on_device(): lax.all_to_all(partial, 'a', split_axis=0, concat_axis=0, tiled=True)  56.8 us
    pallas_call x1, Pallas kernels, tower_step(): pl.pallas_call(functools.partial(tower_kernel, chunk), grid_spec=pltpu.Pr...  53.9 us
    ppermute x4, waiting for transfers between devices, swap(): return lax.ppermute(x, GROUP, [(d, d ^ bit) for d in range(size)])  46.7 us
    all_gather x1, waiting for transfers between devices, on_device(): lax.all_gather(weighted.astype(jnp.bfloat16), 'a', axis=0, tiled=False)  35.2 us
  transfers between devices with their start and end apart: 10, of which 5 were waited for; matrix products, arithmetic and copies ran while one was open for 12% of the time, Pallas kernels for 0%

profile of v1, /device:TPU:0, one launch (start us, length us, event | category | flops | bytes accessed | tf_op | source)
XLA Modules:
  0.0 426.6 jit_solution(8097859577439269818)
XLA Ops:
  7.2 3.0 collective-permute-start
  11.6 5.8 %all-to-all-start = ((bf16[12,8,1,32,128]{4,3,0,2,1:T(8,128)(2,1)}), bf16[12,8,1,32,128]{4,3,0,2,1:T(8,128)(2,1)}, u32[]{:S(2)}, u32[]{:S(2)}) async-start(bf16[12,8,1,32,128]{4,3,0,2,1:T(8,128)(2,1)} %copy.34), calls=%async_computation | async-start | bytes 1572864 | tf_op jit(solution)/shard_map/all_to_all | solution.py:219
  17.5 43.3 %collective-permute-done = bf16[1,1128,1024]{2,1,0:T(8,128)(2,1)} collective-permute-done((bf16[1,1128,1024]{2,1,0:T(8,128)(2,1)}, bf16[1,1128,1024]{2,1,0:T(8,128)(2,1)}, u32[]{:S(2)}, u32[]{:S(2)}) %collective-permute-start) | collective-permute-done | bytes 2310176 | tf_op jit(solution)/shard_map/ppermute | solution.py:41
  60.8 4.2 pad_maximum_fusion.2
  65.8 1.8 gather_fusion.1
  68.9 1.7 fusion.1
  70.7 2.3 copy.35
  73.0 2.3 multiply_convert_fusion.1
  88.0 4.2 pad_maximum_fusion
  92.2 3.6 dynamic-slice_bitcast_fusion.4
  95.8 6.5 %pad_maximum_fusion.1.w_ref = bf16[4512,1024]{1,0:T(8,128)(2,1)} fusion(bf16[1128,1024]{1,0:T(8,128)(2,1)S(1)} %get-tuple-element.33, bf16[1128,1024]{1,0:T(8,128)(2,1)} %get-tuple-element.34, bf16[1128,1024]{1,0:T(8,128)(2,1)} %get-tuple-element.35, bf16[1128,1024]{1,0:T(8,128)(2,1)S(1)} %get-tuple-element.32), kind=kLoop, calls=%fused_computation.3 | loop fusion | flops 36962304 | bytes 18481152 | tf_op jit(solution)/shard_map/concatenate | solution.py:53
  102.3 35.2 %all-gather.7.cloned.1.call-done = bf16[384,32,128]{2,1,0:T(8,128)(2,1)} async-done(((bf16[48,32,128]{2,1,0:T(8,128)(2,1)}), bf16[384,32,128]{2,1,0:T(8,128)(2,1)}) %all-gather.7.cloned.1.call-update) | async-done | bytes 3145744 | tf_op jit(solution)/shard_map/all_gather | solution.py:230
  137.6 53.9 %shard_map.137 = (bf16[4512,1024]{1,0:T(8,128)(2,1)}, bf16[8,48,32,128]{3,2,1,0:T(8,128)(2,1)}, f32[32,32]{1,0:T(8,128)}) custom-call(s32[141]{0:T(256)} %dynamic_slice.29.left_ref, s32[141]{0:T(256)} %dynamic_slice.30.right_ref, bf16[4512,1024]{1,0:T(8,128)(2,1)} %pad_maximum_fusion.1.w_ref, bf16[8,1024,128]{2,1,0:T(8,128)(2,1)} %bitcast.104, ...), custom_call_target="tpu_custom_call" | custom-call | flops 18924699648 | bytes 18481152 | tf_op jit(solution)/shard_map/pallas_call | solution.py:160
  191.5 5.0 %dynamic-slice_bitcast_fusion = bf16[2,1128,1024]{2,1,0:T(8,128)(2,1)} fusion(bf16[2,2,1128,1024]{3,2,1,0:T(8,128)(2,1)} %bitcast.92, s32[]{:T(128)S(6)} %select_n.65), kind=kLoop, calls=%fused_computation.9 | loop fusion | bytes 9240580 | tf_op jit(solution)/shard_map/jit(dynamic_index_in_dim)/squeeze | solution.py:64
  196.4 4.6 %all-to-all-start.1 = ((bf16[8,48,32,128]{3,2,1,0:T(8,128)(2,1)}), bf16[8,48,32,128]{3,2,1,0:T(8,128)(2,1)}, u32[]{:S(2)}, u32[]{:S(2)}) async-start(bf16[8,48,32,128]{3,2,1,0:T(8,128)(2,1)} %get-tuple-element.8), calls=%async_computation.1 | async-start | bytes 6291456 | tf_op jit(solution)/shard_map/all_to_all | solution.py:239
  201.1 3.4 collective-permute-done.2
  204.6 6.0 %fusion = bf16[2,1128,1024]{2,1,0:T(8,128)(2,1)S(1)} fusion(bf16[2,1128,1024]{2,1,0:T(8,128)(2,1)} %collective-permute-done.2, bf16[2,2,1128,1024]{3,2,1,0:T(8,128)(2,1)} %bitcast.93, s32[]{:T(128)S(6)} %select_n.64), kind=kLoop, calls=%fused_computation.5 | loop fusion | flops 9240576 | bytes 13860868 | tf_op jit(solution)/shard_map/convert_element_type | solution.py:67
  210.6 2.1 copy-done.3
  212.7 1.6 constant_dynamic-slice_fusion
  215.8 56.8 %all-to-all-done.1 = bf16[8,48,32,128]{3,2,1,0:T(8,128)(2,1)} async-done(((bf16[8,48,32,128]{3,2,1,0:T(8,128)(2,1)}), bf16[8,48,32,128]{3,2,1,0:T(8,128)(2,1)}, u32[]{:S(2)}, u32[]{:S(2)}) %all-to-all-start.1) | async-done | bytes 3145760 | tf_op jit(solution)/shard_map/all_to_all | solution.py:239
  272.6 2.4 convert_reduce_fusion
  277.9 3.6 all-to-all-start.2
  283.3 127.3 %all-reduce.3.cloned.1.call-done = f32[208,128]{1,0:T(8,128)} async-done(((f32[208,128]{1,0:T(8,128)}), f32[208,128]{1,0:T(8,128)}) %all-reduce.3.cloned.1.call-update) | async-done | bytes 106512 | tf_op jit(solution)/shard_map/psum | solution.py:254
  414.5 5.5 %multiply_bitcast_fusion = f32[1128,1024]{1,0:T(8,128)} fusion(bf16[1,1128,1024]{2,1,0:T(8,128)(2,1)} %collective-permute-done.3, bf16[2,1128,1024]{2,1,0:T(8,128)(2,1)} %copy-done.3, s32[]{:T(128)S(6)} %select_n.67), kind=kLoop, calls=%fused_computation.8 | loop fusion | flops 4620288 | bytes 9240580 | tf_op jit(solution)/shard_map/mul | solution.py:270
  (85 shorter events, 18.3 us)
Async XLA Ops:
  7.2 53.6 %copy-start.4 = (bf16[1128,1024]{1,0:T(8,128)(2,1)S(1)}, bf16[1128,1024]{1,0:T(8,128)(2,1)}, u32[]{:S(2)}) copy-start(bf16[1128,1024]{1,0:T(8,128)(2,1)} %param.15) | copy-start | bytes 6930436
  7.2 95.2 %all-gather.5.cloned.1.call-start = ((), (), s32[]{:S(2)}) async-start(), calls=%async_computation.4 | async-start | bytes 2359296 | tf_op jit(solution)/shard_map/all_gather | solution.py:214
  7.2 53.5 %collective-permute-start = (bf16[1,1128,1024]{2,1,0:T(8,128)(2,1)}, bf16[1,1128,1024]{2,1,0:T(8,128)(2,1)}, u32[]{:S(2)}, u32[]{:S(2)}) collective-permute-start(bf16[1,1128,1024]{2,1,0:T(8,128)(2,1)} %bitcast.94), channel_id=1, source_target_pairs={{0,2},{1,3},{2,0},{3,1},{4,6},{5,7},{6,4},{7,5},{8,10},{9,11},{10,... | collective-permute-start | bytes 6930440 | tf_op jit(solution)/shard_map/ppermute | solution.py:41
  11.6 54.2 %all-to-all-start = ((bf16[12,8,1,32,128]{4,3,0,2,1:T(8,128)(2,1)}), bf16[12,8,1,32,128]{4,3,0,2,1:T(8,128)(2,1)}, u32[]{:S(2)}, u32[]{:S(2)}) async-start(bf16[12,8,1,32,128]{4,3,0,2,1:T(8,128)(2,1)} %copy.34), calls=%async_computation | async-start | bytes 1572864 | tf_op jit(solution)/shard_map/all_to_all | solution.py:219
  17.4 47.6 %copy-start.16 = (s32[48]{0:T(128)S(1)}, s32[48]{0:T(128)}, u32[]{:S(2)}) copy-start(s32[48]{0:T(128)} %param.11) | copy-start | bytes 580
  17.4 51.4 %copy-start.13 = (f32[16,48]{1,0:T(8,128)S(1)}, f32[16,48]{1,0:T(8,128)}, u32[]{:S(2)}) copy-start(f32[16,48]{1,0:T(8,128)} %param.12) | copy-start | bytes 9220
  17.4 51.5 %copy-start.7 = (f32[1536,16]{0,1:T(8,128)S(1)}, f32[1536,16]{0,1:T(8,128)}, u32[]{:S(2)}) copy-start(f32[1536,16]{0,1:T(8,128)} %param.13) | copy-start | bytes 294916
  17.5 120.1 %all-gather.7.cloned.1.call-start = ((), (), s32[]{:S(2)}) async-start(), calls=%async_computation.5 | async-start | bytes 3538944 | tf_op jit(solution)/shard_map/all_gather | solution.py:230
  65.0 10.3 %copy-start.2 = (s32[4]{0:T(128)S(1)}, s32[4]{0:T(128)}, u32[]{:S(2)}) copy-start(s32[4]{0:T(128)} %constant.120.clone) | copy-start | bytes 52
  65.0 19.6 %copy-start.11 = (f32[32,32]{1,0:T(8,128)S(1)}, f32[32,32]{1,0:T(8,128)}, u32[]{:S(2)}) copy-start(f32[32,32]{1,0:T(8,128)} %param.14) | copy-start | bytes 12292
  65.0 22.9 %collective-permute-start.1 = (bf16[2,1128,1024]{2,1,0:T(8,128)(2,1)}, bf16[2,1128,1024]{2,1,0:T(8,128)(2,1)}, u32[]{:S(2)}, u32[]{:S(2)}) collective-permute-start(bf16[2,1128,1024]{2,1,0:T(8,128)(2,1)} %pad_maximum_fusion.2), channel_id=1, source_target_pairs={{0,1},{1,0},{2,3},{3,2},{4,5},{5,4},{6,7},{7,6},{8,9},{9,8},{10,11... | collective-permute-start | bytes 13860872 | tf_op jit(solution)/shard_map/ppermute | solution.py:41
  68.8 19.2 %copy-start.9 = (f32[48,128]{1,0:T(8,128)}, f32[48,128]{1,0:T(8,128)S(1)}, u32[]{:S(2)}) copy-start(f32[48,128]{1,0:T(8,128)S(1)} %get-tuple-element.40) | copy-start | bytes 73732
  196.4 8.1 %collective-permute-start.2 = (bf16[2,1128,1024]{2,1,0:T(8,128)(2,1)}, bf16[2,1128,1024]{2,1,0:T(8,128)(2,1)}, u32[]{:S(2)}, u32[]{:S(2)}) collective-permute-start(bf16[2,1128,1024]{2,1,0:T(8,128)(2,1)} %dynamic-slice_bitcast_fusion), channel_id=1, source_target_pairs={{0,1},{1,0},{2,3},{3,2},{4,5},{5,4},{6,7},{7,6},{8,9},{9,8},{10,11... | collective-permute-start | bytes 13860872 | tf_op jit(solution)/shard_map/ppermute | solution.py:41
  196.4 76.1 %all-to-all-start.1 = ((bf16[8,48,32,128]{3,2,1,0:T(8,128)(2,1)}), bf16[8,48,32,128]{3,2,1,0:T(8,128)(2,1)}, u32[]{:S(2)}, u32[]{:S(2)}) async-start(bf16[8,48,32,128]{3,2,1,0:T(8,128)(2,1)} %get-tuple-element.8), calls=%async_computation.1 | async-start | bytes 6291456 | tf_op jit(solution)/shard_map/all_to_all | solution.py:239
  212.7 62.3 %copy-start.5 = (f32[48,32,128]{2,1,0:T(8,128)S(1)}, f32[48,32,128]{2,1,0:T(8,128)}, u32[]{:S(2)}) copy-start(f32[48,32,128]{2,1,0:T(8,128)} %get-tuple-element.41) | copy-start | bytes 2359300
  212.7 62.4 %copy-start.8 = (f32[1536,16]{0,1:T(8,128)S(1)}, f32[1536,16]{0,1:T(8,128)}, u32[]{:S(2)}) copy-start(f32[1536,16]{0,1:T(8,128)} %param.13) | copy-start | bytes 294916
  214.3 61.6 %copy-start.6 = (f32[1536,128]{1,0:T(8,128)S(1)}, f32[1536,128]{1,0:T(8,128)}, u32[]{:S(2)}) copy-start(f32[1536,128]{1,0:T(8,128)} %copy.35) | copy-start | bytes 2359300
  214.3 61.9 %copy-start.15 = (s32[48]{0:T(128)S(1)}, s32[48]{0:T(128)}, u32[]{:S(2)}) copy-start(s32[48]{0:T(128)} %copy-done.14) | copy-start | bytes 580
  214.3 200.2 %collective-permute-start.3 = (bf16[1,1128,1024]{2,1,0:T(8,128)(2,1)}, bf16[1,1128,1024]{2,1,0:T(8,128)(2,1)}, u32[]{:S(2)}, u32[]{:S(2)}) collective-permute-start(bf16[1,1128,1024]{2,1,0:T(8,128)(2,1)} %constant_dynamic-slice_fusion), channel_id=1, source_target_pairs={{0,2},{1,3},{2,0},{3,1},{4,6},{5,7},{6,4},{7,5},{8,10},{9,11},{10,... | collective-permute-start | bytes 6930440 | tf_op jit(solution)/shard_map/ppermute | solution.py:41
  275.0 6.5 %copy-start.12 = (f32[32,32]{1,0:T(8,128)S(1)}, f32[32,32]{1,0:T(8,128)}, u32[]{:S(2)}) copy-start(f32[32,32]{1,0:T(8,128)} %get-tuple-element.10) | copy-start | bytes 12292
  275.2 7.2 %copy-start.10 = (f32[48,128]{1,0:T(8,128)S(1)}, f32[48,128]{1,0:T(8,128)}, u32[]{:S(2)}) copy-start(f32[48,128]{1,0:T(8,128)} %copy-done.9) | copy-start | bytes 73732
  277.9 135.7 %all-to-all-start.2 = ((bf16[96,1,1,32,128]{4,3,2,1,0:T(8,128)(2,1)}), bf16[96,1,1,32,128]{4,3,2,1,0:T(8,128)(2,1)S(1)}, u32[]{:S(2)}, u32[]{:S(2)}) async-start(bf16[96,1,1,32,128]{4,3,2,1,0:T(8,128)(2,1)} %copy.38), calls=%async_computation.2 | async-start | bytes 1572864 | tf_op jit(solution)/shard_map/all_to_all | solution.py:269
  281.5 129.1 %all-reduce.3.cloned.1.call-start = ((), (), s32[]{:S(2)}) async-start(), calls=%async_computation.3 | async-start | bytes 212992 | tf_op jit(solution)/shard_map/psum | solution.py:254
  413.5 6.5 %copy-start.1 = (bf16[12,8,1,32,128]{4,3,2,1,0:T(8,128)(2,1)S(1)}, bf16[12,8,1,32,128]{4,3,2,1,0:T(8,128)(2,1)}, u32[]{:S(2)}) copy-start(bf16[12,8,1,32,128]{4,3,2,1,0:T(8,128)(2,1)} %param.10) | copy-start | bytes 2359300
  (3 other events, 5.8 us)
Sparse Core Ops, SparseCore 0:
  10.4 60.6 all-gather.4
  75.4 62.1 all-gather.6
  287.9 122.6 all-reduce.2

commit v2 on v1

--- a/solution.py
+++ b/solution.py
@@ -41,16 +41,16 @@
     return lax.ppermute(x, GROUP, [(d, d ^ bit) for d in range(size)])
 
 
-def gather_rows(shard, size, me):
-    held = shard[None]
-    offsets = [0]
+def spread(own, axis, size, after=None):
+    held = {0: own}
     for bit in reversed(bits_of(size)):
-        held = jnp.concatenate([held, swap(held, size, bit)], axis=0)
-        offsets = offsets + [o ^ bit for o in offsets]
-    place = np.argsort(np.array(offsets))
-    order = jnp.asarray(place, jnp.int32)[jnp.arange(size, dtype=jnp.int32) ^ me]
-    parts = [lax.dynamic_index_in_dim(held, order[d], 0, keepdims=False) for d in range(size)]
-    return jnp.concatenate(parts, axis=0)
+        pairs = [(d, d ^ bit) for d in range(size)]
+        for offset in list(held):
+            block = held[offset]
+            if offset and after is not None:
+                block = lax.optimization_barrier((block, after))[0]
+            held[offset ^ bit] = lax.ppermute(block, axis, pairs)
+    return [held[r] for r in range(size)]
 
 
 def scatter_rows(total, size, me):
@@ -69,26 +69,23 @@
 
 
 def tower_kernel(
-    chunk, left_ref, right_ref, w_ref, cot_ref, wt_ref, fwd_ref, bwd_ref,
-    twg_ref, dwt_ref, gb_ref, cot2, mf, dm, dw, pg, prs,
+    chunk, left_ref, right_ref, order_ref, pg_ref, cot_ref, wt_ref, fwd_ref, bwd_ref,
+    twg_ref, dwt_ref, gb_ref, mf, dm, dw, prs,
 ):
     parts, count, width, lanes = wt_ref.shape
     step = pl.program_id(0)
-    depth = cot2.shape[0]
+    depth = cot_ref.shape[0]
     tile = min(256, depth)
-    ntile = min(256, parts * lanes)
+    order = [order_ref[a] for a in range(parts)]
 
     def columns(a):
         return slice(a * lanes, (a + 1) * lanes)
 
     @pl.when(step == 0)
     def _():
-        for a in range(parts):
-            cot2[:, columns(a)] = cot_ref[a]
-
         @pl.loop(0, count)
         def _(f):
-            rows = jnp.concatenate([wt_ref[a, f] for a in range(parts)], axis=1)
+            rows = jnp.concatenate([wt_ref[order[a], f] for a in range(parts)], axis=1)
             both = jnp.dot(fwd_ref[...], rows, preferred_element_type=jnp.float32)
             value = both[:width] + both[width:]
             for a in range(parts):
@@ -96,19 +93,14 @@
                 dm[a, f] = jnp.zeros((width, lanes), jnp.float32)
                 dw[a, f] = jnp.zeros((width, lanes), jnp.float32)
 
-    @pl.loop(0, parts * lanes // ntile)
-    def _(c):
-        cols = pl.ds(pl.multiple_of(c * ntile, ntile), ntile)
-        pg[:, cols] = jnp.dot(w_ref[...], cot2[:, cols], preferred_element_type=jnp.float32)
-
     @pl.loop(0, chunk)
     def _(q):
         i = left_ref[step * chunk + q]
         j = right_ref[step * chunk + q]
         rows = pl.ds(pl.multiple_of(q * width, width), width)
         for a in range(parts):
-            g = pg[rows, columns(a)]
-            w = wt_ref[a, j].astype(jnp.float32)
+            g = pg_ref[rows, columns(a)].astype(jnp.float32)
+            w = wt_ref[order[a], j].astype(jnp.float32)
             m = mf[a, i]
             prs[rows, columns(a)] = (m * w).astype(jnp.bfloat16)
             dm[a, i] += g * w
@@ -118,7 +110,7 @@
     def _(c):
         cols = pl.ds(pl.multiple_of(c * tile, tile), tile)
         twg_ref[:, cols] = lax.dot_general(
-            prs[...], cot2[cols, :], (((1,), (1,)), ((), ())), preferred_element_type=jnp.float32
+            prs[...], cot_ref[cols, :], (((1,), (1,)), ((), ())), preferred_element_type=jnp.float32
         ).astype(jnp.bfloat16)
 
     @pl.when(step == pl.num_programs(0) - 1)
@@ -128,11 +120,11 @@
         @pl.loop(0, count)
         def _(f):
             d = jnp.concatenate([dm[a, f].astype(jnp.bfloat16) for a in range(parts)], axis=1)
-            rows = jnp.concatenate([wt_ref[a, f] for a in range(parts)], axis=1)
+            rows = jnp.concatenate([wt_ref[order[a], f] for a in range(parts)], axis=1)
             both = jnp.dot(bwd_ref[...], d, preferred_element_type=jnp.float32)
             value = both[:width] + both[width:]
             for a in range(parts):
-                dwt_ref[a, f] = (dw[a, f] + value[:, columns(a)]).astype(jnp.bfloat16)
+                dwt_ref[order[a], f] = (dw[a, f] + value[:, columns(a)]).astype(jnp.bfloat16)
             gb_ref[...] += lax.dot_general(
                 rows, d, (((1,), (1,)), ((), ())), preferred_element_type=jnp.float32
             )
@@ -144,9 +136,9 @@
     return jnp.concatenate([top, rest], axis=0)
 
 
-def tower_step(left, right, weights, cot, weighted, w_bilinear):
+def tower_step(left, right, order, pair_grad, cot, weighted, w_bilinear):
     parts, count, width, lanes = weighted.shape
-    depth = cot.shape[1]
+    depth = cot.shape[0]
     pairs = left.shape[0]
     steps = next(c for c in (3, 2, 4, 5, 6, 7, 1) if pairs % c == 0)
     chunk = pairs // steps
@@ -160,10 +152,10 @@
     return pl.pallas_call(
         functools.partial(tower_kernel, chunk),
         grid_spec=pltpu.PrefetchScalarGridSpec(
-            num_scalar_prefetch=2,
+            num_scalar_prefetch=3,
             grid=(steps,),
             in_specs=[
-                pl.BlockSpec((rows, depth), lambda s, *_: (s, 0)),
+                pl.BlockSpec((rows, samples), lambda s, *_: (s, 0)),
                 whole(cot.shape),
                 whole(big),
                 whole((2 * width, width)),
@@ -175,11 +167,9 @@
                 whole((width, width)),
             ],
             scratch_shapes=[
-                pltpu.VMEM((depth, samples), jnp.bfloat16),
                 pltpu.VMEM(big, jnp.float32),
                 pltpu.VMEM(big, jnp.float32),
                 pltpu.VMEM(big, jnp.float32),
-                pltpu.VMEM((rows, samples), jnp.float32),
                 pltpu.VMEM((rows, samples), jnp.bfloat16),
             ],
         ),
@@ -192,11 +182,11 @@
             dimension_semantics=("arbitrary",), vmem_limit_bytes=60 * 1024 * 1024
         ),
         cost_estimate=pl.CostEstimate(
-            flops=4 * pairs * width * depth * samples,
+            flops=2 * pairs * width * depth * samples,
             bytes_accessed=4 * pairs * width * depth,
             transcendentals=0,
         ),
-    )(left, right, weights, cot, weighted, two_parts(w_bilinear.T), two_parts(w_bilinear))
+    )(left, right, order, pair_grad, cot, weighted, two_parts(w_bilinear.T), two_parts(w_bilinear))
 
 
 def on_device(pooled, field_owner, w_squeeze, w_excite, w_bilinear, tower_weight, tower_cotangent):
@@ -209,9 +199,6 @@
     me = lax.axis_index("l") * subs + lax.axis_index("sub")
     scale = 1.0 / width**0.5
     signs = hadamard_table(width)
-
-    weights = gather_rows(tower_weight, size, me)
-    cot = lax.all_gather(tower_cotangent, "a", axis=0, tiled=False)
 
     rotated = (
         jnp.einsum("ij,ktsjb->ktsib", signs, pooled, preferred_element_type=jnp.float32) * scale
@@ -227,14 +214,27 @@
     activated = raw * gate
     excite = jnp.dot(w_excite, activated, precision=HIGH).reshape(count, width, samples)
     weighted = fields * (1.0 + excite)
-    weighted_all = lax.all_gather(weighted.astype(jnp.bfloat16), "a", axis=0, tiled=False)
+    narrow = weighted.astype(jnp.bfloat16)
+    weighted_all = lax.all_gather(narrow, "a", axis=0, tiled=False)
+
+    mine_a = lax.axis_index("a")
+    order = jnp.arange(parts, dtype=jnp.int32) ^ mine_a
+    cot = jnp.concatenate(spread(tower_cotangent, "a", parts, narrow), axis=1)
+    shards = spread(tower_weight, GROUP, size, narrow)
+    rows = tower_weight.shape[0]
+    pair_grad = jnp.zeros((size * rows, cot.shape[1]), jnp.bfloat16)
+    for offset, shard in enumerate(shards):
+        block = jnp.dot(shard, cot, preferred_element_type=jnp.float32).astype(jnp.bfloat16)
+        pair_grad = lax.dynamic_update_slice_in_dim(pair_grad, block, (me ^ offset) * rows, 0)
 
     table_left, table_right = np.triu_indices(count, 1)
     mine = table_left.shape[0] // parts
-    start = lax.axis_index("a") * mine
+    start = mine_a * mine
     left = lax.dynamic_slice_in_dim(jnp.asarray(table_left, jnp.int32), start, mine)
     right = lax.dynamic_slice_in_dim(jnp.asarray(table_right, jnp.int32), start, mine)
-    totals, partial, d_bilinear = tower_step(left, right, weights, cot, weighted_all, w_bilinear)
+    totals, partial, d_bilinear = tower_step(
+        left, right, order, pair_grad, cot, weighted_all, w_bilinear
+    )
 
     arrived = lax.all_to_all(partial, "a", split_axis=0, concat_axis=0, tiled=True)
     d_weighted = jnp.sum(arrived.astype(jnp.float32), axis=0)
@@ -249,9 +249,12 @@
     field_grad = d_weighted * (1.0 + excite) + (d_squeezed * (1.0 / width))[:, None, :]
 
     flat = jnp.concatenate([g_excite.reshape(-1), g_squeeze.reshape(-1), d_bilinear.reshape(-1)])
-    flat = jnp.pad(flat, (0, -flat.shape[0] % 1024)).reshape(-1, 128)
-    inverse = 1.0 / (tables * subs * samples)
-    flat = (lax.psum(flat, EVERY) * inverse).reshape(-1)
+    devices = tables * subs
+    inverse = 1.0 / (devices * samples)
+    flat = jnp.pad(flat, (0, -flat.shape[0] % (devices * 1024))).reshape(devices, -1, 128)
+    share = jnp.sum(lax.all_to_all(flat, EVERY, 0, 0, tiled=True), axis=0) * inverse
+    share = jnp.broadcast_to(share[None], flat.shape)
+    flat = lax.all_to_all(share, EVERY, 0, 0, tiled=True).reshape(-1)
     n_excite, n_squeeze = count * width * hidden, hidden * count
     g_excite = flat[:n_excite].reshape(hidden, count * width).T
     g_squeeze = flat[n_excite : n_excite + n_squeeze].reshape(hidden, count)

time: 428 us -> 310 us (0.72)
  waiting for transfers between devices: 266 us -> 149 us
  matrix products: 5.54 us -> 23.3 us
  other arithmetic: 34 us -> 17.4 us
  starting transfers between devices: 18.7 us -> 33.6 us
  Pallas kernels: 53.9 us -> 42.1 us
  between operations: 22 us -> 14.3 us
    psum x1 -> x0, waiting for transfers between devices: 127 us -> none  [on_device(): flat = (lax.psum(flat, EVERY) * inverse).reshape(-1)]
    ppermute x4 -> x2, waiting for transfers between devices: 46.7 us -> 2.37 us  [swap(): return lax.ppermute(x, GROUP, [(d, d ^ bit) for d in range(size)])]
    ppermute x0 -> x10, waiting for transfers between devices: none -> 35.6 us  [spread(): held[offset ^ bit] = lax.ppermute(block, axis, pairs)]
    all_gather x2 -> x1, waiting for transfers between devices: 35.2 us -> 0.01 us  [on_device(): weighted_all = lax.all_gather(narrow, 'a', axis=0, tiled=False)]
    all_to_all x1, waiting for transfers between devices: 0.01 us -> 19.9 us  [on_device(): lax.all_to_all(rotated, TABLE, split_axis=1, concat_axis=0, tiled=True)]
    dot_general x0 -> x4, matrix products: none -> 19.5 us  [on_device(): jnp.dot(shard, cot, preferred_element_type=jnp.float32).astype(jnp.bfloat16)]
    all_to_all x1, waiting for transfers between devices: 0.01 us -> 18.6 us  [on_device(): lax.all_to_all(placed, TABLE, split_axis=0, concat_axis=1, tiled=True)]
    concatenate x3 -> x0, other arithmetic: 15 us -> none  [the longest x2 8.42 us: gather_rows(): held = jnp.concatenate([held, swap(held, size, bit)], axis=0)]
  transfers between devices with their start and end apart: 10 -> 18, of which waited for: 5 -> 10; matrix products, arithmetic and copies ran while one was open for 12% -> 17% of each run, Pallas kernels for 0% -> 0%
where the time goes in v2:
time: 310 us; the launch traced here: 309 us
  waiting for transfers between devices  149 us (48%)
  Pallas kernels  42.1 us (14%)
  starting transfers between devices  33.6 us (11%)
  local copies, waits for them, and re-layouts  29.3 us (9%)
  matrix products  23.3 us (8%)
  other arithmetic  17.4 us (6%)
  between operations  14.3 us (5%)
    all_to_all x1, waiting for transfers between devices, on_device(): lax.all_to_all(partial, 'a', split_axis=0, concat_axis=0, tiled=True)  58 us
    pallas_call x1, Pallas kernels, tower_step(): pl.pallas_call(functools.partial(tower_kernel, chunk), grid_spec=pltpu.Pr...  42.1 us
    ppermute x10, waiting for transfers between devices, spread(): held[offset ^ bit] = lax.ppermute(block, axis, pairs)  35.6 us
    all_to_all x1, waiting for transfers between devices, on_device(): lax.all_to_all(rotated, TABLE, split_axis=1, concat_axis=0, tiled=True)  19.9 us
    dot_general x4, matrix products, on_device(): jnp.dot(shard, cot, preferred_element_type=jnp.float32).astype(jnp.bfloat16)  19.5 us
    all_to_all x1, waiting for transfers between devices, on_device(): lax.all_to_all(placed, TABLE, split_axis=0, concat_axis=1, tiled=True)  18.6 us
    ppermute x10, starting transfers between devices, spread(): held[offset ^ bit] = lax.ppermute(block, axis, pairs)  9.17 us
    unnamed x31, local copies, waits for them, and re-layouts  8.38 us
  transfers between devices with their start and end apart: 18, of which 10 were waited for; matrix products, arithmetic and copies ran while one was open for 17% of the time, Pallas kernels for 0%

profile of v2, /device:TPU:0, one launch (start us, length us, event | category | flops | bytes accessed | tf_op | source)
XLA Modules:
  0.0 308.9 jit_solution(4221376909681806478)
XLA Ops:
  9.7 7.2 %all-to-all-start = ((bf16[12,8,1,32,128]{4,3,0,2,1:T(8,128)(2,1)}), bf16[12,8,1,32,128]{4,3,0,2,1:T(8,128)(2,1)S(1)}, u32[]{:S(2)}, u32[]{:S(2)}) async-start(bf16[12,8,1,32,128]{4,3,0,2,1:T(8,128)(2,1)} %copy.33), calls=%async_computation | async-start | bytes 1572864 | tf_op jit(solution)/shard_map/all_to_all | solution.py:206
  17.2 19.9 %all-to-all-done = bf16[12,8,1,32,128]{4,3,0,2,1:T(8,128)(2,1)S(1)} async-done(((bf16[12,8,1,32,128]{4,3,0,2,1:T(8,128)(2,1)}), bf16[12,8,1,32,128]{4,3,0,2,1:T(8,128)(2,1)S(1)}, u32[]{:S(2)}, u32[]{:S(2)}) %all-to-all-start) | async-done | bytes 786464 | tf_op jit(solution)/shard_map/all_to_all | solution.py:206
  46.7 10.5 %collective-permute-done.1 = bf16[1024,128]{1,0:T(8,128)(2,1)S(1)} collective-permute-done((bf16[1024,128]{1,0:T(8,128)(2,1)S(1)}, bf16[1024,128]{1,0:T(8,128)(2,1)S(1)}, u32[]{:S(2)}, u32[]{:S(2)}) %collective-permute-start.1) | collective-permute-done | bytes 262176 | tf_op jit(solution)/shard_map/ppermute | solution.py:52
  57.2 3.5 %collective-permute-start.2 = (bf16[1024,128]{1,0:T(8,128)(2,1)S(1)}, bf16[1024,128]{1,0:T(8,128)(2,1)S(1)}, u32[]{:S(2)}, u32[]{:S(2)}) collective-permute-start(bf16[1024,128]{1,0:T(8,128)(2,1)S(1)} %collective-permute-done.1), channel_id=1, source_target_pairs={{0,4},{4,0},{8,12},{12,8},{16,20},{20,16},{24,28},{28,24},{1,5},{5... | collective-permute-start | bytes 786440 | tf_op jit(solution)/shard_map/ppermute | solution.py:52
  60.7 4.5 %collective-permute-done.3 = bf16[1024,128]{1,0:T(8,128)(2,1)S(1)} collective-permute-done((bf16[1024,128]{1,0:T(8,128)(2,1)S(1)}, bf16[1024,128]{1,0:T(8,128)(2,1)S(1)}, u32[]{:S(2)}, u32[]{:S(2)}) %collective-permute-start.3) | collective-permute-done | bytes 262176 | tf_op jit(solution)/shard_map/ppermute | solution.py:52
  69.9 5.8 %collective-permute-done.5 = bf16[1024,128]{1,0:T(8,128)(2,1)S(1)} collective-permute-done((bf16[1024,128]{1,0:T(8,128)(2,1)S(1)}, bf16[1024,128]{1,0:T(8,128)(2,1)S(1)}, u32[]{:S(2)}, u32[]{:S(2)}) %collective-permute-start.5) | collective-permute-done | bytes 262176 | tf_op jit(solution)/shard_map/ppermute | solution.py:52
  76.4 14.7 %collective-permute-done.8 = bf16[1128,1024]{1,0:T(8,128)(2,1)} collective-permute-done((bf16[1128,1024]{1,0:T(8,128)(2,1)}, bf16[1128,1024]{1,0:T(8,128)(2,1)}, u32[]{:S(2)}, u32[]{:S(2)}) %collective-permute-start.8) | collective-permute-done | bytes 2310176 | tf_op jit(solution)/shard_map/ppermute | solution.py:52
  94.8 4.8 %broadcast_in_dim.16 = bf16[4512,1024]{1,0:T(8,128)(2,1)} broadcast(bf16[]{:T(256)} %constant.94.clone.1), dimensions={} | broadcast | bytes 9240578 | tf_op jit(solution)/shard_map/broadcast_in_dim | solution.py:225
  99.6 4.0 %fusion.3 = bf16[4512,1024]{1,0:T(8,128)(2,1)} fusion(bf16[4512,1024]{1,0:T(8,128)(2,1)} %broadcast_in_dim.16, s32[]{:T(128)S(6)} %select_n.48, bf16[1024,1024]{1,0:T(8,128)(2,1)S(1)} %copy-done.6, bf16[1128,1024]{1,0:T(8,128)(2,1)S(1)} %copy-done.10), kind=kOutput, calls=%fused_computation.12 | convolution fusion | flops 2366742528 | bytes 6717444 | tf_op jit(solution)/shard_map/dot_general | solution.py:227
  103.6 5.7 %fusion.5 = bf16[4512,1024]{1,0:T(8,128)(2,1)} fusion(bf16[4512,1024]{1,0:T(8,128)(2,1)} %fusion.3, s32[]{:T(128)S(6)} %select_n.49, bf16[1024,1024]{1,0:T(8,128)(2,1)S(1)} %copy-done.6, bf16[1128,1024]{1,0:T(8,128)(2,1)} %collective-permute-done.7), kind=kOutput, calls=%fused_computation.14 | convolution fusion | flops 2366742528 | bytes 6717444 | tf_op jit(solution)/shard_map/dot_general | solution.py:227
  109.3 5.6 %fusion.7 = bf16[4512,1024]{1,0:T(8,128)(2,1)} fusion(bf16[4512,1024]{1,0:T(8,128)(2,1)} %fusion.5, s32[]{:T(128)S(6)} %select_n.50, bf16[1024,1024]{1,0:T(8,128)(2,1)S(1)} %copy-done.6, bf16[1128,1024]{1,0:T(8,128)(2,1)} %collective-permute-done.8), kind=kOutput, calls=%fused_computation.16 | convolution fusion | flops 2366742528 | bytes 6717444 | tf_op jit(solution)/shard_map/dot_general | solution.py:227
  114.9 4.2 %fusion.1.pg_ref = bf16[4512,1024]{1,0:T(8,128)(2,1)} fusion(bf16[4512,1024]{1,0:T(8,128)(2,1)} %fusion.7, s32[]{:T(128)S(6)} %select_n.51, bf16[1128,1024]{1,0:T(8,128)(2,1)S(1)} %collective-permute-done.9, bf16[1024,1024]{1,0:T(8,128)(2,1)S(1)} %copy-done.6), kind=kOutput, calls=%fused_computation.7 | convolution fusion | flops 2366742528 | bytes 6717444 | tf_op jit(solution)/shard_map/dot_general | solution.py:227
  119.1 42.1 %shard_map.128 = (bf16[4512,1024]{1,0:T(8,128)(2,1)}, bf16[8,48,32,128]{3,2,1,0:T(8,128)(2,1)}, f32[32,32]{1,0:T(8,128)}) custom-call(s32[141]{0:T(256)} %dynamic_slice.16.left_ref, s32[141]{0:T(256)} %dynamic_slice.17.right_ref, s32[8]{0:T(128)} %iota_xor_fusion.order_ref, bf16[4512,1024]{1,0:T(8,128)(2,1)} %fusion.1.pg_ref, ...), custom_call_target="tpu_custom_call" | custom-call | flops 9462349824 | bytes 18481152 | tf_op jit(solution)/shard_map/pallas_call | solution.py:152
  161.2 5.0 %dynamic-slice_bitcast_fusion = bf16[2,1128,1024]{2,1,0:T(8,128)(2,1)} fusion(bf16[2,2,1128,1024]{3,2,1,0:T(8,128)(2,1)} %bitcast.97, s32[]{:T(128)S(6)} %select_n.53), kind=kLoop, calls=%fused_computation.5 | loop fusion | bytes 9240580 | tf_op jit(solution)/shard_map/jit(dynamic_index_in_dim)/squeeze | solution.py:64
  166.7 5.3 %all-to-all-start.1 = ((bf16[8,48,32,128]{3,2,1,0:T(8,128)(2,1)}), bf16[8,48,32,128]{3,2,1,0:T(8,128)(2,1)}, u32[]{:S(2)}, u32[]{:S(2)}) async-start(bf16[8,48,32,128]{3,2,1,0:T(8,128)(2,1)} %get-tuple-element.16), calls=%async_computation.1 | async-start | bytes 6291456 | tf_op jit(solution)/shard_map/all_to_all | solution.py:239
  174.4 6.0 %fusion = bf16[2,1128,1024]{2,1,0:T(8,128)(2,1)S(1)} fusion(bf16[2,1128,1024]{2,1,0:T(8,128)(2,1)} %collective-permute-done.10, bf16[2,2,1128,1024]{3,2,1,0:T(8,128)(2,1)} %bitcast.98, s32[]{:T(128)S(6)} %select_n.52), kind=kLoop, calls=%fused_computation.2 | loop fusion | flops 9240576 | bytes 13860868 | tf_op jit(solution)/shard_map/convert_element_type | solution.py:67
  184.9 58.0 %all-to-all-done.1 = bf16[8,48,32,128]{3,2,1,0:T(8,128)(2,1)} async-done(((bf16[8,48,32,128]{3,2,1,0:T(8,128)(2,1)}), bf16[8,48,32,128]{3,2,1,0:T(8,128)(2,1)}, u32[]{:S(2)}, u32[]{:S(2)}) %all-to-all-start.1) | async-done | bytes 3145760 | tf_op jit(solution)/shard_map/all_to_all | solution.py:239
  247.7 3.7 %all-to-all-start.3 = ((f32[32,8,128]{2,1,0:T(8,128)}), f32[32,8,128]{2,1,0:T(8,128)S(1)}, u32[]{:S(2)}, u32[]{:S(2)}) async-start(f32[32,8,128]{2,1,0:T(8,128)} %fusion.19), calls=%async_computation.3 | async-start | bytes 262144 | tf_op jit(solution)/shard_map/all_to_all | solution.py:255
  251.6 8.0 %all-to-all-done.3 = f32[32,8,128]{2,1,0:T(8,128)S(1)} async-done(((f32[32,8,128]{2,1,0:T(8,128)}), f32[32,8,128]{2,1,0:T(8,128)S(1)}, u32[]{:S(2)}, u32[]{:S(2)}) %all-to-all-start.3) | async-done | bytes 131104 | tf_op jit(solution)/shard_map/all_to_all | solution.py:255
  260.4 2.6 all-to-all-start.4
  264.8 6.3 %all-to-all-done.4 = f32[32,8,128]{2,1,0:T(8,128)S(1)} async-done(((f32[32,8,128]{2,1,0:T(8,128)}), f32[32,8,128]{2,1,0:T(8,128)S(1)}, u32[]{:S(2)}, u32[]{:S(2)}) %all-to-all-start.4) | async-done | bytes 131104 | tf_op jit(solution)/shard_map/all_to_all | solution.py:257
  271.2 3.5 %all-to-all-start.2 = ((bf16[96,1,1,32,128]{4,3,2,1,0:T(8,128)(2,1)}), bf16[96,1,1,32,128]{4,3,2,1,0:T(8,128)(2,1)S(1)}, u32[]{:S(2)}, u32[]{:S(2)}) async-start(bf16[96,1,1,32,128]{4,3,2,1,0:T(8,128)(2,1)} %copy.37), calls=%async_computation.2 | async-start | bytes 1572864 | tf_op jit(solution)/shard_map/all_to_all | solution.py:272
  276.9 18.6 %all-to-all-done.2 = bf16[96,1,1,32,128]{4,3,2,1,0:T(8,128)(2,1)S(1)} async-done(((bf16[96,1,1,32,128]{4,3,2,1,0:T(8,128)(2,1)}), bf16[96,1,1,32,128]{4,3,2,1,0:T(8,128)(2,1)S(1)}, u32[]{:S(2)}, u32[]{:S(2)}) %all-to-all-start.2) | async-done | bytes 786464 | tf_op jit(solution)/shard_map/all_to_all | solution.py:272
  296.4 5.6 %multiply_bitcast_fusion = f32[1128,1024]{1,0:T(8,128)} fusion(bf16[1,1128,1024]{2,1,0:T(8,128)(2,1)} %collective-permute-done.11, bf16[2,1128,1024]{2,1,0:T(8,128)(2,1)} %copy-done.2, s32[]{:T(128)S(6)} %select_n.55), kind=kLoop, calls=%fused_computation.4 | loop fusion | flops 4620288 | bytes 9240580 | tf_op jit(solution)/shard_map/mul | solution.py:273
  (95 shorter events, 39.3 us)
Async XLA Ops:
  7.2 9.8 %copy-start.9 = (s32[48]{0:T(128)S(1)}, s32[48]{0:T(128)}, u32[]{:S(2)}) copy-start(s32[48]{0:T(128)} %param.10) | copy-start | bytes 580
  8.7 29.4 %copy-start.8 = (f32[16,48]{1,0:T(8,128)S(1)}, f32[16,48]{1,0:T(8,128)}, u32[]{:S(2)}) copy-start(f32[16,48]{1,0:T(8,128)} %param.11) | copy-start | bytes 9220
  8.7 29.5 %copy-start.3 = (f32[1536,16]{0,1:T(8,128)S(1)}, f32[1536,16]{0,1:T(8,128)}, u32[]{:S(2)}) copy-start(f32[1536,16]{0,1:T(8,128)} %param.12) | copy-start | bytes 294916
  9.7 27.4 %all-to-all-start = ((bf16[12,8,1,32,128]{4,3,0,2,1:T(8,128)(2,1)}), bf16[12,8,1,32,128]{4,3,0,2,1:T(8,128)(2,1)S(1)}, u32[]{:S(2)}, u32[]{:S(2)}) async-start(bf16[12,8,1,32,128]{4,3,0,2,1:T(8,128)(2,1)} %copy.33), calls=%async_computation | async-start | bytes 1572864 | tf_op jit(solution)/shard_map/all_to_all | solution.py:206
  16.9 102.2 %all-gather.3.cloned.1.call-start = ((), (), s32[]{:S(2)}) async-start(), calls=%async_computation.5 | async-start | bytes 3538944 | tf_op jit(solution)/shard_map/all_gather | solution.py:218
  38.2 7.1 %copy-start.5 = (f32[32,32]{1,0:T(8,128)S(1)}, f32[32,32]{1,0:T(8,128)}, u32[]{:S(2)}) copy-start(f32[32,32]{1,0:T(8,128)} %param.13) | copy-start | bytes 12292
  40.3 50.9 %collective-permute-start.8 = (bf16[1128,1024]{1,0:T(8,128)(2,1)}, bf16[1128,1024]{1,0:T(8,128)(2,1)}, u32[]{:S(2)}, u32[]{:S(2)}) collective-permute-start(bf16[1128,1024]{1,0:T(8,128)(2,1)} %param.14), channel_id=1, source_target_pairs={{0,2},{1,3},{2,0},{3,1},{4,6},{5,7},{6,4},{7,5},{8,10},{9,11},{10,... | collective-permute-start | bytes 6930440 | tf_op jit(solution)/shard_map/ppermute | solution.py:52
  41.8 61.7 %collective-permute-start.7 = (bf16[1128,1024]{1,0:T(8,128)(2,1)}, bf16[1128,1024]{1,0:T(8,128)(2,1)}, u32[]{:S(2)}, u32[]{:S(2)}) collective-permute-start(bf16[1128,1024]{1,0:T(8,128)(2,1)} %param.14), channel_id=1, source_target_pairs={{0,1},{1,0},{2,3},{3,2},{4,5},{5,4},{6,7},{7,6},{8,9},{9,8},{10,11... | collective-permute-start | bytes 6930440 | tf_op jit(solution)/shard_map/ppermute | solution.py:52
  41.9 15.4 %collective-permute-start.1 = (bf16[1024,128]{1,0:T(8,128)(2,1)S(1)}, bf16[1024,128]{1,0:T(8,128)(2,1)S(1)}, u32[]{:S(2)}, u32[]{:S(2)}) collective-permute-start(bf16[1024,128]{1,0:T(8,128)(2,1)S(1)} %copy-done.4), channel_id=1, source_target_pairs={{0,8},{4,12},{8,0},{12,4},{16,24},{20,28},{24,16},{28,20},{1,9},{5... | collective-permute-start | bytes 786440 | tf_op jit(solution)/shard_map/ppermute | solution.py:52
  42.2 26.3 %collective-permute-start = (bf16[1024,128]{1,0:T(8,128)(2,1)S(1)}, bf16[1024,128]{1,0:T(8,128)(2,1)S(1)}, u32[]{:S(2)}, u32[]{:S(2)}) collective-permute-start(bf16[1024,128]{1,0:T(8,128)(2,1)S(1)} %copy-done.4), channel_id=1, source_target_pairs={{0,4},{4,0},{8,12},{12,8},{16,20},{20,16},{24,28},{28,24},{1,5},{5... | collective-permute-start | bytes 786440 | tf_op jit(solution)/shard_map/ppermute | solution.py:52
  43.3 21.9 %collective-permute-start.3 = (bf16[1024,128]{1,0:T(8,128)(2,1)S(1)}, bf16[1024,128]{1,0:T(8,128)(2,1)S(1)}, u32[]{:S(2)}, u32[]{:S(2)}) collective-permute-start(bf16[1024,128]{1,0:T(8,128)(2,1)S(1)} %copy-done.4), channel_id=1, source_target_pairs={{0,16},{4,20},{8,24},{12,28},{16,0},{20,4},{24,8},{28,12},{1,17},{... | collective-permute-start | bytes 786440 | tf_op jit(solution)/shard_map/ppermute | solution.py:52
  57.2 33.9 %collective-permute-start.2 = (bf16[1024,128]{1,0:T(8,128)(2,1)S(1)}, bf16[1024,128]{1,0:T(8,128)(2,1)S(1)}, u32[]{:S(2)}, u32[]{:S(2)}) collective-permute-start(bf16[1024,128]{1,0:T(8,128)(2,1)S(1)} %collective-permute-done.1), channel_id=1, source_target_pairs={{0,4},{4,0},{8,12},{12,8},{16,20},{20,16},{24,28},{28,24},{1,5},{5... | collective-permute-start | bytes 786440 | tf_op jit(solution)/shard_map/ppermute | solution.py:52
  65.2 10.5 %collective-permute-start.5 = (bf16[1024,128]{1,0:T(8,128)(2,1)S(1)}, bf16[1024,128]{1,0:T(8,128)(2,1)S(1)}, u32[]{:S(2)}, u32[]{:S(2)}) collective-permute-start(bf16[1024,128]{1,0:T(8,128)(2,1)S(1)} %collective-permute-done.3), channel_id=1, source_target_pairs={{0,8},{4,12},{8,0},{12,4},{16,24},{20,28},{24,16},{28,20},{1,9},{5... | collective-permute-start | bytes 786440 | tf_op jit(solution)/shard_map/ppermute | solution.py:52
  69.2 23.4 %collective-permute-start.4 = (bf16[1024,128]{1,0:T(8,128)(2,1)S(1)}, bf16[1024,128]{1,0:T(8,128)(2,1)S(1)}, u32[]{:S(2)}, u32[]{:S(2)}) collective-permute-start(bf16[1024,128]{1,0:T(8,128)(2,1)S(1)} %collective-permute-done.3), channel_id=1, source_target_pairs={{0,4},{4,0},{8,12},{12,8},{16,20},{20,16},{24,28},{28,24},{1,5},{5... | collective-permute-start | bytes 786440 | tf_op jit(solution)/shard_map/ppermute | solution.py:52
  75.8 18.3 %collective-permute-start.6 = (bf16[1024,128]{1,0:T(8,128)(2,1)S(1)}, bf16[1024,128]{1,0:T(8,128)(2,1)S(1)}, u32[]{:S(2)}, u32[]{:S(2)}) collective-permute-start(bf16[1024,128]{1,0:T(8,128)(2,1)S(1)} %collective-permute-done.5), channel_id=1, source_target_pairs={{0,4},{4,0},{8,12},{12,8},{16,20},{20,16},{24,28},{28,24},{1,5},{5... | collective-permute-start | bytes 786440 | tf_op jit(solution)/shard_map/ppermute | solution.py:52
  91.2 23.7 %collective-permute-start.9 = (bf16[1128,1024]{1,0:T(8,128)(2,1)}, bf16[1128,1024]{1,0:T(8,128)(2,1)S(1)}, u32[]{:S(2)}, u32[]{:S(2)}) collective-permute-start(bf16[1128,1024]{1,0:T(8,128)(2,1)} %collective-permute-done.8), channel_id=1, source_target_pairs={{0,1},{1,0},{2,3},{3,2},{4,5},{5,4},{6,7},{7,6},{8,9},{9,8},{10,11... | collective-permute-start | bytes 6930440 | tf_op jit(solution)/shard_map/ppermute | solution.py:52
  166.1 8.3 %collective-permute-start.10 = (bf16[2,1128,1024]{2,1,0:T(8,128)(2,1)}, bf16[2,1128,1024]{2,1,0:T(8,128)(2,1)}, u32[]{:S(2)}, u32[]{:S(2)}) collective-permute-start(bf16[2,1128,1024]{2,1,0:T(8,128)(2,1)} %dynamic-slice_bitcast_fusion), channel_id=1, source_target_pairs={{0,1},{1,0},{2,3},{3,2},{4,5},{5,4},{6,7},{7,6},{8,9},{9,8},{10,11... | collective-permute-start | bytes 13860872 | tf_op jit(solution)/shard_map/ppermute | solution.py:41
  166.7 5.3 %copy-start.7 = (f32[32,32]{1,0:T(8,128)S(1)}, f32[32,32]{1,0:T(8,128)}, u32[]{:S(2)}) copy-start(f32[32,32]{1,0:T(8,128)} %get-tuple-element.18) | copy-start | bytes 12292
  166.7 76.3 %all-to-all-start.1 = ((bf16[8,48,32,128]{3,2,1,0:T(8,128)(2,1)}), bf16[8,48,32,128]{3,2,1,0:T(8,128)(2,1)}, u32[]{:S(2)}, u32[]{:S(2)}) async-start(bf16[8,48,32,128]{3,2,1,0:T(8,128)(2,1)} %get-tuple-element.16), calls=%async_computation.1 | async-start | bytes 6291456 | tf_op jit(solution)/shard_map/all_to_all | solution.py:239
  183.4 113.0 %collective-permute-start.11 = (bf16[1,1128,1024]{2,1,0:T(8,128)(2,1)}, bf16[1,1128,1024]{2,1,0:T(8,128)(2,1)}, u32[]{:S(2)}, u32[]{:S(2)}) collective-permute-start(bf16[1,1128,1024]{2,1,0:T(8,128)(2,1)} %constant_dynamic-slice_fusion), channel_id=1, source_target_pairs={{0,2},{1,3},{2,0},{3,1},{4,6},{5,7},{6,4},{7,5},{8,10},{9,11},{10,... | collective-permute-start | bytes 6930440 | tf_op jit(solution)/shard_map/ppermute | solution.py:41
  247.7 11.9 %all-to-all-start.3 = ((f32[32,8,128]{2,1,0:T(8,128)}), f32[32,8,128]{2,1,0:T(8,128)S(1)}, u32[]{:S(2)}, u32[]{:S(2)}) async-start(f32[32,8,128]{2,1,0:T(8,128)} %fusion.19), calls=%async_computation.3 | async-start | bytes 262144 | tf_op jit(solution)/shard_map/all_to_all | solution.py:255
  260.4 10.8 %all-to-all-start.4 = ((f32[32,8,128]{2,1,0:T(8,128)}), f32[32,8,128]{2,1,0:T(8,128)S(1)}, u32[]{:S(2)}, u32[]{:S(2)}) async-start(f32[32,8,128]{2,1,0:T(8,128)} %broadcast_in_dim.34), calls=%async_computation.4 | async-start | bytes 262144 | tf_op jit(solution)/shard_map/all_to_all | solution.py:257
  271.2 24.3 %all-to-all-start.2 = ((bf16[96,1,1,32,128]{4,3,2,1,0:T(8,128)(2,1)}), bf16[96,1,1,32,128]{4,3,2,1,0:T(8,128)(2,1)S(1)}, u32[]{:S(2)}, u32[]{:S(2)}) async-start(bf16[96,1,1,32,128]{4,3,2,1,0:T(8,128)(2,1)} %copy.37), calls=%async_computation.2 | async-start | bytes 1572864 | tf_op jit(solution)/shard_map/all_to_all | solution.py:272
  296.4 5.6 %copy-start.1 = (bf16[12,8,1,32,128]{4,3,2,1,0:T(8,128)(2,1)S(1)}, bf16[12,8,1,32,128]{4,3,2,1,0:T(8,128)(2,1)}, u32[]{:S(2)}) copy-start(bf16[12,8,1,32,128]{4,3,2,1,0:T(8,128)(2,1)} %param.9) | copy-start | bytes 2359300
  (5 other events, 17.3 us)
Sparse Core Ops, SparseCore 0:
  40.4 69.6 all-gather.2

commit v3 on v2

--- a/solution.py
+++ b/solution.py
@@ -219,10 +219,10 @@
 
     mine_a = lax.axis_index("a")
     order = jnp.arange(parts, dtype=jnp.int32) ^ mine_a
+    rows = tower_weight.shape[0]
     cot = jnp.concatenate(spread(tower_cotangent, "a", parts, narrow), axis=1)
     shards = spread(tower_weight, GROUP, size, narrow)
-    rows = tower_weight.shape[0]
-    pair_grad = jnp.zeros((size * rows, cot.shape[1]), jnp.bfloat16)
+    pair_grad = jnp.zeros((size * rows, parts * samples), jnp.bfloat16)
     for offset, shard in enumerate(shards):
         block = jnp.dot(shard, cot, preferred_element_type=jnp.float32).astype(jnp.bfloat16)
         pair_grad = lax.dynamic_update_slice_in_dim(pair_grad, block, (me ^ offset) * rows, 0)
@@ -247,19 +247,6 @@
     g_squeeze = lax.dot_general(d_raw, squeezed, (((1,), (1,)), ((), ())), precision=HIGH)
     d_squeezed = lax.dot_general(w_squeeze, d_raw, (((0,), (0,)), ((), ())), precision=HIGH)
     field_grad = d_weighted * (1.0 + excite) + (d_squeezed * (1.0 / width))[:, None, :]
-
-    flat = jnp.concatenate([g_excite.reshape(-1), g_squeeze.reshape(-1), d_bilinear.reshape(-1)])
-    devices = tables * subs
-    inverse = 1.0 / (devices * samples)
-    flat = jnp.pad(flat, (0, -flat.shape[0] % (devices * 1024))).reshape(devices, -1, 128)
-    share = jnp.sum(lax.all_to_all(flat, EVERY, 0, 0, tiled=True), axis=0) * inverse
-    share = jnp.broadcast_to(share[None], flat.shape)
-    flat = lax.all_to_all(share, EVERY, 0, 0, tiled=True).reshape(-1)
-    n_excite, n_squeeze = count * width * hidden, hidden * count
-    g_excite = flat[:n_excite].reshape(hidden, count * width).T
-    g_squeeze = flat[n_excite : n_excite + n_squeeze].reshape(hidden, count)
-    at = n_excite + n_squeeze
-    g_bilinear = flat[at : at + width * width].reshape(width, width)
 
     slot_count = per_owner * tables
     onehot = (slot_index[None, :] == jnp.arange(slot_count, dtype=jnp.int32)[:, None]).astype(
@@ -270,6 +257,22 @@
     ).astype(jnp.bfloat16)
     placed = placed.reshape(slot_count, 1, 1, width, samples)
     row_grads = lax.all_to_all(placed, TABLE, split_axis=0, concat_axis=1, tiled=True)
+
+    flat = jnp.concatenate([g_excite.reshape(-1), g_squeeze.reshape(-1), d_bilinear.reshape(-1)])
+    devices = tables * subs
+    inverse = 1.0 / (devices * samples)
+    devices = tables * subs
+    inverse = 1.0 / (devices * samples)
+    flat = jnp.pad(flat, (0, -flat.shape[0] % 1024)).reshape(-1, 128) * inverse
+    flat = lax.optimization_barrier((flat, placed))[0]
+    for bit in bits_of(devices):
+        flat = flat + lax.ppermute(flat, EVERY, [(d, d ^ bit) for d in range(devices)])
+    flat = flat.reshape(-1)
+    n_excite, n_squeeze = count * width * hidden, hidden * count
+    g_excite = flat[:n_excite].reshape(hidden, count * width).T
+    g_squeeze = flat[n_excite : n_excite + n_squeeze].reshape(hidden, count)
+    at = n_excite + n_squeeze
+    g_bilinear = flat[at : at + width * width].reshape(width, width)
     return (row_grads, weight_total * inverse, g_squeeze, g_excite, g_bilinear)
 
 

time: 310 us -> 297 us (0.958)
  waiting for transfers between devices: 149 us -> 137 us
    ppermute x0 -> x5, waiting for transfers between devices: none -> 21.1 us  [on_device(): lax.ppermute(flat, EVERY, [(d, d ^ bit) for d in range(devices)])]
    all_to_all x1, waiting for transfers between devices: 18.6 us -> 0.01 us  [on_device(): lax.all_to_all(placed, TABLE, split_axis=0, concat_axis=1, tiled=True)]
    all_to_all x2 -> x0, waiting for transfers between devices: 14.3 us -> none  [the longest x1 8 us: on_device(): lax.all_to_all(flat, EVERY, 0, 0, tiled=True)]
    ppermute x0 -> x5, starting transfers between devices: none -> 7.38 us  [on_device(): lax.ppermute(flat, EVERY, [(d, d ^ bit) for d in range(devices)])]
    all_to_all x2 -> x0, starting transfers between devices: 6.25 us -> none  [the longest x1 3.68 us: on_device(): lax.all_to_all(flat, EVERY, 0, 0, tiled=True)]
  transfers between devices with their start and end apart: 18 -> 21, of which waited for: 10 -> 12; matrix products, arithmetic and copies ran while one was open for 17% -> 17% of each run, Pallas kernels for 0% -> 0%
where the time goes in v3:
time: 297 us
  waiting for transfers between devices  137 us (46%)
  Pallas kernels  42.1 us (14%)
  starting transfers between devices  34.6 us (12%)
  local copies, waits for them, and re-layouts  28.5 us (10%)
  matrix products  23.3 us (8%)
  other arithmetic  16.8 us (6%)
  between operations  14.3 us (5%)
    all_to_all x1, waiting for transfers between devices, on_device(): lax.all_to_all(partial, 'a', split_axis=0, concat_axis=0, tiled=True)  57.9 us
    pallas_call x1, Pallas kernels, tower_step(): pl.pallas_call(functools.partial(tower_kernel, chunk), grid_spec=pltpu.Pr...  42.1 us
    ppermute x10, waiting for transfers between devices, spread(): held[offset ^ bit] = lax.ppermute(block, axis, pairs)  35.7 us
    ppermute x5, waiting for transfers between devices, on_device(): lax.ppermute(flat, EVERY, [(d, d ^ bit) for d in range(devices)])  21.1 us
    all_to_all x1, waiting for transfers between devices, on_device(): lax.all_to_all(rotated, TABLE, split_axis=1, concat_axis=0, tiled=True)  19.9 us
    dot_general x4, matrix products, on_device(): jnp.dot(shard, cot, preferred_element_type=jnp.float32).astype(jnp.bfloat16)  19.6 us
    ppermute x10, starting transfers between devices, spread(): held[offset ^ bit] = lax.ppermute(block, axis, pairs)  9.16 us
    unnamed x31, local copies, waits for them, and re-layouts  8.35 us
  transfers between devices with their start and end apart: 21, of which 12 were waited for; matrix products, arithmetic and copies ran while one was open for 17% of the time, Pallas kernels for 0%

profile of v3, /device:TPU:0, one launch (start us, length us, event | category | flops | bytes accessed | tf_op | source)
XLA Modules:
  0.0 296.9 jit_solution(6464557926081565170)
XLA Ops:
  9.7 7.2 %all-to-all-start = ((bf16[12,8,1,32,128]{4,3,0,2,1:T(8,128)(2,1)}), bf16[12,8,1,32,128]{4,3,0,2,1:T(8,128)(2,1)S(1)}, u32[]{:S(2)}, u32[]{:S(2)}) async-start(bf16[12,8,1,32,128]{4,3,0,2,1:T(8,128)(2,1)} %copy.33), calls=%async_computation | async-start | bytes 1572864 | tf_op jit(solution)/shard_map/all_to_all | solution.py:206
  17.2 19.9 %all-to-all-done = bf16[12,8,1,32,128]{4,3,0,2,1:T(8,128)(2,1)S(1)} async-done(((bf16[12,8,1,32,128]{4,3,0,2,1:T(8,128)(2,1)}), bf16[12,8,1,32,128]{4,3,0,2,1:T(8,128)(2,1)S(1)}, u32[]{:S(2)}, u32[]{:S(2)}) %all-to-all-start) | async-done | bytes 786464 | tf_op jit(solution)/shard_map/all_to_all | solution.py:206
  46.7 10.5 %collective-permute-done.1 = bf16[1024,128]{1,0:T(8,128)(2,1)S(1)} collective-permute-done((bf16[1024,128]{1,0:T(8,128)(2,1)S(1)}, bf16[1024,128]{1,0:T(8,128)(2,1)S(1)}, u32[]{:S(2)}, u32[]{:S(2)}) %collective-permute-start.1) | collective-permute-done | bytes 262176 | tf_op jit(solution)/shard_map/ppermute | solution.py:52
  57.2 3.5 %collective-permute-start.2 = (bf16[1024,128]{1,0:T(8,128)(2,1)S(1)}, bf16[1024,128]{1,0:T(8,128)(2,1)S(1)}, u32[]{:S(2)}, u32[]{:S(2)}) collective-permute-start(bf16[1024,128]{1,0:T(8,128)(2,1)S(1)} %collective-permute-done.1), channel_id=1, source_target_pairs={{0,4},{4,0},{8,12},{12,8},{16,20},{20,16},{24,28},{28,24},{1,5},{5... | collective-permute-start | bytes 786440 | tf_op jit(solution)/shard_map/ppermute | solution.py:52
  60.7 4.5 %collective-permute-done.3 = bf16[1024,128]{1,0:T(8,128)(2,1)S(1)} collective-permute-done((bf16[1024,128]{1,0:T(8,128)(2,1)S(1)}, bf16[1024,128]{1,0:T(8,128)(2,1)S(1)}, u32[]{:S(2)}, u32[]{:S(2)}) %collective-permute-start.3) | collective-permute-done | bytes 262176 | tf_op jit(solution)/shard_map/ppermute | solution.py:52
  69.9 5.9 %collective-permute-done.5 = bf16[1024,128]{1,0:T(8,128)(2,1)S(1)} collective-permute-done((bf16[1024,128]{1,0:T(8,128)(2,1)S(1)}, bf16[1024,128]{1,0:T(8,128)(2,1)S(1)}, u32[]{:S(2)}, u32[]{:S(2)}) %collective-permute-start.5) | collective-permute-done | bytes 262176 | tf_op jit(solution)/shard_map/ppermute | solution.py:52
  76.4 14.7 %collective-permute-done.8 = bf16[1128,1024]{1,0:T(8,128)(2,1)} collective-permute-done((bf16[1128,1024]{1,0:T(8,128)(2,1)}, bf16[1128,1024]{1,0:T(8,128)(2,1)}, u32[]{:S(2)}, u32[]{:S(2)}) %collective-permute-start.8) | collective-permute-done | bytes 2310176 | tf_op jit(solution)/shard_map/ppermute | solution.py:52
  94.8 4.8 %broadcast_in_dim.14 = bf16[4512,1024]{1,0:T(8,128)(2,1)} broadcast(bf16[]{:T(256)} %constant.94.clone.1), dimensions={} | broadcast | bytes 9240578 | tf_op jit(solution)/shard_map/broadcast_in_dim | solution.py:225
  99.6 4.0 %fusion.3 = bf16[4512,1024]{1,0:T(8,128)(2,1)} fusion(bf16[4512,1024]{1,0:T(8,128)(2,1)} %broadcast_in_dim.14, s32[]{:T(128)S(6)} %select_n.48, bf16[1024,1024]{1,0:T(8,128)(2,1)S(1)} %copy-done.6, bf16[1128,1024]{1,0:T(8,128)(2,1)S(1)} %copy-done.10), kind=kOutput, calls=%fused_computation.12 | convolution fusion | flops 2366742528 | bytes 6717444 | tf_op jit(solution)/shard_map/dot_general | solution.py:227
  103.6 5.7 %fusion.5 = bf16[4512,1024]{1,0:T(8,128)(2,1)} fusion(bf16[4512,1024]{1,0:T(8,128)(2,1)} %fusion.3, s32[]{:T(128)S(6)} %select_n.49, bf16[1024,1024]{1,0:T(8,128)(2,1)S(1)} %copy-done.6, bf16[1128,1024]{1,0:T(8,128)(2,1)} %collective-permute-done.7), kind=kOutput, calls=%fused_computation.14 | convolution fusion | flops 2366742528 | bytes 6717444 | tf_op jit(solution)/shard_map/dot_general | solution.py:227
  109.3 5.7 %fusion.7 = bf16[4512,1024]{1,0:T(8,128)(2,1)} fusion(bf16[4512,1024]{1,0:T(8,128)(2,1)} %fusion.5, s32[]{:T(128)S(6)} %select_n.50, bf16[1024,1024]{1,0:T(8,128)(2,1)S(1)} %copy-done.6, bf16[1128,1024]{1,0:T(8,128)(2,1)} %collective-permute-done.8), kind=kOutput, calls=%fused_computation.16 | convolution fusion | flops 2366742528 | bytes 6717444 | tf_op jit(solution)/shard_map/dot_general | solution.py:227
  114.9 4.2 %fusion.1.pg_ref = bf16[4512,1024]{1,0:T(8,128)(2,1)} fusion(bf16[4512,1024]{1,0:T(8,128)(2,1)} %fusion.7, s32[]{:T(128)S(6)} %select_n.51, bf16[1128,1024]{1,0:T(8,128)(2,1)S(1)} %collective-permute-done.9, bf16[1024,1024]{1,0:T(8,128)(2,1)S(1)} %copy-done.6), kind=kOutput, calls=%fused_computation.7 | convolution fusion | flops 2366742528 | bytes 6717444 | tf_op jit(solution)/shard_map/dot_general | solution.py:227
  119.1 42.1 %shard_map.128 = (bf16[4512,1024]{1,0:T(8,128)(2,1)}, bf16[8,48,32,128]{3,2,1,0:T(8,128)(2,1)}, f32[32,32]{1,0:T(8,128)}) custom-call(s32[141]{0:T(256)} %dynamic_slice.16.left_ref, s32[141]{0:T(256)} %dynamic_slice.17.right_ref, s32[8]{0:T(128)} %iota_xor_fusion.order_ref, bf16[4512,1024]{1,0:T(8,128)(2,1)} %fusion.1.pg_ref, ...), custom_call_target="tpu_custom_call" | custom-call | flops 9462349824 | bytes 18481152 | tf_op jit(solution)/shard_map/pallas_call | solution.py:152
  161.2 5.0 %dynamic-slice_bitcast_fusion = bf16[2,1128,1024]{2,1,0:T(8,128)(2,1)} fusion(bf16[2,2,1128,1024]{3,2,1,0:T(8,128)(2,1)} %bitcast.96, s32[]{:T(128)S(6)} %select_n.53), kind=kLoop, calls=%fused_computation.5 | loop fusion | bytes 9240580 | tf_op jit(solution)/shard_map/jit(dynamic_index_in_dim)/squeeze | solution.py:64
  166.7 5.1 %all-to-all-start.1 = ((bf16[8,48,32,128]{3,2,1,0:T(8,128)(2,1)}), bf16[8,48,32,128]{3,2,1,0:T(8,128)(2,1)}, u32[]{:S(2)}, u32[]{:S(2)}) async-start(bf16[8,48,32,128]{3,2,1,0:T(8,128)(2,1)} %get-tuple-element.17), calls=%async_computation.1 | async-start | bytes 6291456 | tf_op jit(solution)/shard_map/all_to_all | solution.py:239
  174.4 6.0 %fusion = bf16[2,1128,1024]{2,1,0:T(8,128)(2,1)S(1)} fusion(bf16[2,1128,1024]{2,1,0:T(8,128)(2,1)} %collective-permute-done.10, bf16[2,2,1128,1024]{3,2,1,0:T(8,128)(2,1)} %bitcast.97, s32[]{:T(128)S(6)} %select_n.52), kind=kLoop, calls=%fused_computation.2 | loop fusion | flops 9240576 | bytes 13860868 | tf_op jit(solution)/shard_map/convert_element_type | solution.py:67
  184.9 57.9 %all-to-all-done.1 = bf16[8,48,32,128]{3,2,1,0:T(8,128)(2,1)} async-done(((bf16[8,48,32,128]{3,2,1,0:T(8,128)(2,1)}), bf16[8,48,32,128]{3,2,1,0:T(8,128)(2,1)}, u32[]{:S(2)}, u32[]{:S(2)}) %all-to-all-start.1) | async-done | bytes 3145760 | tf_op jit(solution)/shard_map/all_to_all | solution.py:239
  248.1 3.6 %all-to-all-start.2 = ((bf16[96,1,1,32,128]{4,3,2,1,0:T(8,128)(2,1)}), bf16[96,1,1,32,128]{4,3,2,1,0:T(8,128)(2,1)S(1)}, u32[]{:S(2)}, u32[]{:S(2)}) async-start(bf16[96,1,1,32,128]{4,3,2,1,0:T(8,128)(2,1)} %copy.37), calls=%async_computation.2 | async-start | bytes 1572864 | tf_op jit(solution)/shard_map/all_to_all | solution.py:259
  255.8 3.5 %collective-permute-done.13 = f32[208,128]{1,0:T(8,128)S(1)} collective-permute-done((f32[208,128]{1,0:T(8,128)S(1)}, f32[208,128]{1,0:T(8,128)S(1)}, u32[]{:S(2)}, u32[]{:S(2)}) %collective-permute-start.13) | collective-permute-done | bytes 106528 | tf_op jit(solution)/shard_map/ppermute | solution.py:269
  261.4 3.5 %collective-permute-done.14 = f32[208,128]{1,0:T(8,128)S(1)} collective-permute-done((f32[208,128]{1,0:T(8,128)S(1)}, f32[208,128]{1,0:T(8,128)S(1)}, u32[]{:S(2)}, u32[]{:S(2)}) %collective-permute-start.14) | collective-permute-done | bytes 106528 | tf_op jit(solution)/shard_map/ppermute | solution.py:269
  264.9 3.6 %collective-permute-start.15 = (f32[208,128]{1,0:T(8,128)S(1)}, f32[208,128]{1,0:T(8,128)S(1)}, u32[]{:S(2)}, u32[]{:S(2)}) collective-permute-start(f32[208,128]{1,0:T(8,128)S(1)} %add.116), channel_id=1, source_target_pairs={{0,8},{1,9},{2,10},{3,11},{4,12},{5,13},{6,14},{7,15},{8,0},{9,1},... | collective-permute-start | bytes 319496 | tf_op jit(solution)/shard_map/ppermute | solution.py:269
  268.5 5.8 %collective-permute-done.15 = f32[208,128]{1,0:T(8,128)S(1)} collective-permute-done((f32[208,128]{1,0:T(8,128)S(1)}, f32[208,128]{1,0:T(8,128)S(1)}, u32[]{:S(2)}, u32[]{:S(2)}) %collective-permute-start.15) | collective-permute-done | bytes 106528 | tf_op jit(solution)/shard_map/ppermute | solution.py:269
  274.4 7.0 %collective-permute-done.16 = f32[208,128]{1,0:T(8,128)S(1)} collective-permute-done((f32[208,128]{1,0:T(8,128)S(1)}, f32[208,128]{1,0:T(8,128)S(1)}, u32[]{:S(2)}, u32[]{:S(2)}) %collective-permute-start.16) | collective-permute-done | bytes 106528 | tf_op jit(solution)/shard_map/ppermute | solution.py:269
  284.4 5.6 %multiply_bitcast_fusion = f32[1128,1024]{1,0:T(8,128)} fusion(bf16[1,1128,1024]{2,1,0:T(8,128)(2,1)} %collective-permute-done.11, bf16[2,1128,1024]{2,1,0:T(8,128)(2,1)} %copy-done.2, s32[]{:T(128)S(6)} %select_n.55), kind=kLoop, calls=%fused_computation.4 | loop fusion | flops 4620288 | bytes 9240580 | tf_op jit(solution)/shard_map/mul | solution.py:276
  (103 shorter events, 43.2 us)
Async XLA Ops:
  7.2 9.8 %copy-start.9 = (s32[48]{0:T(128)S(1)}, s32[48]{0:T(128)}, u32[]{:S(2)}) copy-start(s32[48]{0:T(128)} %param.10) | copy-start | bytes 580
  8.7 29.4 %copy-start.8 = (f32[16,48]{1,0:T(8,128)S(1)}, f32[16,48]{1,0:T(8,128)}, u32[]{:S(2)}) copy-start(f32[16,48]{1,0:T(8,128)} %param.11) | copy-start | bytes 9220
  8.7 29.5 %copy-start.3 = (f32[1536,16]{0,1:T(8,128)S(1)}, f32[1536,16]{0,1:T(8,128)}, u32[]{:S(2)}) copy-start(f32[1536,16]{0,1:T(8,128)} %param.12) | copy-start | bytes 294916
  9.7 27.4 %all-to-all-start = ((bf16[12,8,1,32,128]{4,3,0,2,1:T(8,128)(2,1)}), bf16[12,8,1,32,128]{4,3,0,2,1:T(8,128)(2,1)S(1)}, u32[]{:S(2)}, u32[]{:S(2)}) async-start(bf16[12,8,1,32,128]{4,3,0,2,1:T(8,128)(2,1)} %copy.33), calls=%async_computation | async-start | bytes 1572864 | tf_op jit(solution)/shard_map/all_to_all | solution.py:206
  16.9 102.2 %all-gather.3.cloned.1.call-start = ((), (), s32[]{:S(2)}) async-start(), calls=%async_computation.3 | async-start | bytes 3538944 | tf_op jit(solution)/shard_map/all_gather | solution.py:218
  40.3 50.9 %collective-permute-start.8 = (bf16[1128,1024]{1,0:T(8,128)(2,1)}, bf16[1128,1024]{1,0:T(8,128)(2,1)}, u32[]{:S(2)}, u32[]{:S(2)}) collective-permute-start(bf16[1128,1024]{1,0:T(8,128)(2,1)} %param.14), channel_id=1, source_target_pairs={{0,2},{1,3},{2,0},{3,1},{4,6},{5,7},{6,4},{7,5},{8,10},{9,11},{10,... | collective-permute-start | bytes 6930440 | tf_op jit(solution)/shard_map/ppermute | solution.py:52
  41.8 61.7 %collective-permute-start.7 = (bf16[1128,1024]{1,0:T(8,128)(2,1)}, bf16[1128,1024]{1,0:T(8,128)(2,1)}, u32[]{:S(2)}, u32[]{:S(2)}) collective-permute-start(bf16[1128,1024]{1,0:T(8,128)(2,1)} %param.14), channel_id=1, source_target_pairs={{0,1},{1,0},{2,3},{3,2},{4,5},{5,4},{6,7},{7,6},{8,9},{9,8},{10,11... | collective-permute-start | bytes 6930440 | tf_op jit(solution)/shard_map/ppermute | solution.py:52
  41.9 15.4 %collective-permute-start.1 = (bf16[1024,128]{1,0:T(8,128)(2,1)S(1)}, bf16[1024,128]{1,0:T(8,128)(2,1)S(1)}, u32[]{:S(2)}, u32[]{:S(2)}) collective-permute-start(bf16[1024,128]{1,0:T(8,128)(2,1)S(1)} %copy-done.4), channel_id=1, source_target_pairs={{0,8},{4,12},{8,0},{12,4},{16,24},{20,28},{24,16},{28,20},{1,9},{5... | collective-permute-start | bytes 786440 | tf_op jit(solution)/shard_map/ppermute | solution.py:52
  42.2 26.2 %collective-permute-start = (bf16[1024,128]{1,0:T(8,128)(2,1)S(1)}, bf16[1024,128]{1,0:T(8,128)(2,1)S(1)}, u32[]{:S(2)}, u32[]{:S(2)}) collective-permute-start(bf16[1024,128]{1,0:T(8,128)(2,1)S(1)} %copy-done.4), channel_id=1, source_target_pairs={{0,4},{4,0},{8,12},{12,8},{16,20},{20,16},{24,28},{28,24},{1,5},{5... | collective-permute-start | bytes 786440 | tf_op jit(solution)/shard_map/ppermute | solution.py:52
  43.3 21.9 %collective-permute-start.3 = (bf16[1024,128]{1,0:T(8,128)(2,1)S(1)}, bf16[1024,128]{1,0:T(8,128)(2,1)S(1)}, u32[]{:S(2)}, u32[]{:S(2)}) collective-permute-start(bf16[1024,128]{1,0:T(8,128)(2,1)S(1)} %copy-done.4), channel_id=1, source_target_pairs={{0,16},{4,20},{8,24},{12,28},{16,0},{20,4},{24,8},{28,12},{1,17},{... | collective-permute-start | bytes 786440 | tf_op jit(solution)/shard_map/ppermute | solution.py:52
  57.2 33.9 %collective-permute-start.2 = (bf16[1024,128]{1,0:T(8,128)(2,1)S(1)}, bf16[1024,128]{1,0:T(8,128)(2,1)S(1)}, u32[]{:S(2)}, u32[]{:S(2)}) collective-permute-start(bf16[1024,128]{1,0:T(8,128)(2,1)S(1)} %collective-permute-done.1), channel_id=1, source_target_pairs={{0,4},{4,0},{8,12},{12,8},{16,20},{20,16},{24,28},{28,24},{1,5},{5... | collective-permute-start | bytes 786440 | tf_op jit(solution)/shard_map/ppermute | solution.py:52
  65.2 10.5 %collective-permute-start.5 = (bf16[1024,128]{1,0:T(8,128)(2,1)S(1)}, bf16[1024,128]{1,0:T(8,128)(2,1)S(1)}, u32[]{:S(2)}, u32[]{:S(2)}) collective-permute-start(bf16[1024,128]{1,0:T(8,128)(2,1)S(1)} %collective-permute-done.3), channel_id=1, source_target_pairs={{0,8},{4,12},{8,0},{12,4},{16,24},{20,28},{24,16},{28,20},{1,9},{5... | collective-permute-start | bytes 786440 | tf_op jit(solution)/shard_map/ppermute | solution.py:52
  69.2 23.5 %collective-permute-start.4 = (bf16[1024,128]{1,0:T(8,128)(2,1)S(1)}, bf16[1024,128]{1,0:T(8,128)(2,1)S(1)}, u32[]{:S(2)}, u32[]{:S(2)}) collective-permute-start(bf16[1024,128]{1,0:T(8,128)(2,1)S(1)} %collective-permute-done.3), channel_id=1, source_target_pairs={{0,4},{4,0},{8,12},{12,8},{16,20},{20,16},{24,28},{28,24},{1,5},{5... | collective-permute-start | bytes 786440 | tf_op jit(solution)/shard_map/ppermute | solution.py:52
  75.8 18.3 %collective-permute-start.6 = (bf16[1024,128]{1,0:T(8,128)(2,1)S(1)}, bf16[1024,128]{1,0:T(8,128)(2,1)S(1)}, u32[]{:S(2)}, u32[]{:S(2)}) collective-permute-start(bf16[1024,128]{1,0:T(8,128)(2,1)S(1)} %collective-permute-done.5), channel_id=1, source_target_pairs={{0,4},{4,0},{8,12},{12,8},{16,20},{20,16},{24,28},{28,24},{1,5},{5... | collective-permute-start | bytes 786440 | tf_op jit(solution)/shard_map/ppermute | solution.py:52
  91.2 23.8 %collective-permute-start.9 = (bf16[1128,1024]{1,0:T(8,128)(2,1)}, bf16[1128,1024]{1,0:T(8,128)(2,1)S(1)}, u32[]{:S(2)}, u32[]{:S(2)}) collective-permute-start(bf16[1128,1024]{1,0:T(8,128)(2,1)} %collective-permute-done.8), channel_id=1, source_target_pairs={{0,1},{1,0},{2,3},{3,2},{4,5},{5,4},{6,7},{7,6},{8,9},{9,8},{10,11... | collective-permute-start | bytes 6930440 | tf_op jit(solution)/shard_map/ppermute | solution.py:52
  166.2 8.2 %collective-permute-start.10 = (bf16[2,1128,1024]{2,1,0:T(8,128)(2,1)}, bf16[2,1128,1024]{2,1,0:T(8,128)(2,1)}, u32[]{:S(2)}, u32[]{:S(2)}) collective-permute-start(bf16[2,1128,1024]{2,1,0:T(8,128)(2,1)} %dynamic-slice_bitcast_fusion), channel_id=1, source_target_pairs={{0,1},{1,0},{2,3},{3,2},{4,5},{5,4},{6,7},{7,6},{8,9},{9,8},{10,11... | collective-permute-start | bytes 13860872 | tf_op jit(solution)/shard_map/ppermute | solution.py:41
  166.7 76.1 %all-to-all-start.1 = ((bf16[8,48,32,128]{3,2,1,0:T(8,128)(2,1)}), bf16[8,48,32,128]{3,2,1,0:T(8,128)(2,1)}, u32[]{:S(2)}, u32[]{:S(2)}) async-start(bf16[8,48,32,128]{3,2,1,0:T(8,128)(2,1)} %get-tuple-element.17), calls=%async_computation.1 | async-start | bytes 6291456 | tf_op jit(solution)/shard_map/all_to_all | solution.py:239
  183.4 101.0 %collective-permute-start.11 = (bf16[1,1128,1024]{2,1,0:T(8,128)(2,1)}, bf16[1,1128,1024]{2,1,0:T(8,128)(2,1)}, u32[]{:S(2)}, u32[]{:S(2)}) collective-permute-start(bf16[1,1128,1024]{2,1,0:T(8,128)(2,1)} %constant_dynamic-slice_fusion), channel_id=1, source_target_pairs={{0,2},{1,3},{2,0},{3,1},{4,6},{5,7},{6,4},{7,5},{8,10},{9,11},{10,... | collective-permute-start | bytes 6930440 | tf_op jit(solution)/shard_map/ppermute | solution.py:41
  248.1 35.4 %all-to-all-start.2 = ((bf16[96,1,1,32,128]{4,3,2,1,0:T(8,128)(2,1)}), bf16[96,1,1,32,128]{4,3,2,1,0:T(8,128)(2,1)S(1)}, u32[]{:S(2)}, u32[]{:S(2)}) async-start(bf16[96,1,1,32,128]{4,3,2,1,0:T(8,128)(2,1)} %copy.37), calls=%async_computation.2 | async-start | bytes 1572864 | tf_op jit(solution)/shard_map/all_to_all | solution.py:259
  252.8 1.4 collective-permute-start.12
  254.2 5.1 %collective-permute-start.13 = (f32[208,128]{1,0:T(8,128)S(1)}, f32[208,128]{1,0:T(8,128)S(1)}, u32[]{:S(2)}, u32[]{:S(2)}) collective-permute-start(f32[208,128]{1,0:T(8,128)S(1)} %add.114), channel_id=1, source_target_pairs={{0,2},{1,3},{2,0},{3,1},{4,6},{5,7},{6,4},{7,5},{8,10},{9,11},{10,... | collective-permute-start | bytes 319496 | tf_op jit(solution)/shard_map/ppermute | solution.py:269
  259.3 5.6 %collective-permute-start.14 = (f32[208,128]{1,0:T(8,128)S(1)}, f32[208,128]{1,0:T(8,128)S(1)}, u32[]{:S(2)}, u32[]{:S(2)}) collective-permute-start(f32[208,128]{1,0:T(8,128)S(1)} %add.115), channel_id=1, source_target_pairs={{0,4},{1,5},{2,6},{3,7},{4,0},{5,1},{6,2},{7,3},{8,12},{9,13},{10,... | collective-permute-start | bytes 319496 | tf_op jit(solution)/shard_map/ppermute | solution.py:269
  264.9 9.4 %collective-permute-start.15 = (f32[208,128]{1,0:T(8,128)S(1)}, f32[208,128]{1,0:T(8,128)S(1)}, u32[]{:S(2)}, u32[]{:S(2)}) collective-permute-start(f32[208,128]{1,0:T(8,128)S(1)} %add.116), channel_id=1, source_target_pairs={{0,8},{1,9},{2,10},{3,11},{4,12},{5,13},{6,14},{7,15},{8,0},{9,1},... | collective-permute-start | bytes 319496 | tf_op jit(solution)/shard_map/ppermute | solution.py:269
  274.3 7.0 %collective-permute-start.16 = (f32[208,128]{1,0:T(8,128)S(1)}, f32[208,128]{1,0:T(8,128)S(1)}, u32[]{:S(2)}, u32[]{:S(2)}) collective-permute-start(f32[208,128]{1,0:T(8,128)S(1)} %add.117), channel_id=1, source_target_pairs={{0,16},{1,17},{2,18},{3,19},{4,20},{5,21},{6,22},{7,23},{8,24},{9,... | collective-permute-start | bytes 319496 | tf_op jit(solution)/shard_map/ppermute | solution.py:269
  (8 other events, 35.3 us)
Sparse Core Ops, SparseCore 0:
  40.4 69.6 all-gather.2
